TPU v7x, 32 devices: a whole 2x2x4 slice. The times are simulated.
32 devices in a mesh: dp: 4 (over z), fsdp: 8 (over y, x, core).
Axes of the slice: x: 2, y: 2, z: 4, core: 2. Of those that a mesh axis runs over, the one named last changes fastest.
Arguments:
- patches: bfloat16 [4, 32, 1024, 768], P(None, ('dp', 'fsdp')), may hold values from -6 to 6
- labels: int32 [4, 32], P(None, ('dp', 'fsdp')), may hold values from 0 to 999
- valid: int32 [4, 32], P(None, ('dp', 'fsdp')), may hold values from 0 to 1, as said below
- mat3: float32 [320, 2560], P('fsdp'), may hold values from -0.3125 to 0.3125
- tall3: float32 [3328, 320], P('fsdp'), may hold values from -0.15625 to 0.15625
- mat4: float32 [512, 5096], P('fsdp'), may hold values from -0.25 to 0.25
- tall4: float32 [3328, 512], P('fsdp'), may hold values from -0.15625 to 0.15625
- depth: float32 [9, 3328], P(None, 'fsdp'), may hold values from -2 to 2
- norms3: float32 [8, 320], P(None, 'fsdp')
- norms4: float32 [8, 512], P(None, 'fsdp')
- mom_mat3: float32 [320, 2560], P('fsdp'), may hold values from -2.3841858e-07 to 2.3841858e-07
- mom_tall3: float32 [3328, 320], P('fsdp'), may hold values from -2.3841858e-07 to 2.3841858e-07
- mom_mat4: float32 [512, 5096], P('fsdp'), may hold values from -2.3841858e-07 to 2.3841858e-07
- mom_tall4: float32 [3328, 512], P('fsdp'), may hold values from -2.3841858e-07 to 2.3841858e-07
- mom_depth: float32 [9, 3328], P(None, 'fsdp'), may hold values from -2.3841858e-07 to 2.3841858e-07
- mom_norms3: float32 [8, 320], P(None, 'fsdp'), may hold values from -2.3841858e-07 to 2.3841858e-07
- mom_norms4: float32 [8, 512], P(None, 'fsdp'), may hold values from -2.3841858e-07 to 2.3841858e-07
- sq_mat3: float32 [320, 2560], P('fsdp'), may hold values from 1.6041436e-16 to 6.416574e-16
- sq_tall3: float32 [3328, 320], P('fsdp'), may hold values from 1.6041436e-16 to 6.416574e-16
- sq_mat4: float32 [512, 5096], P('fsdp'), may hold values from 1.6041436e-16 to 6.416574e-16
- sq_tall4: float32 [3328, 512], P('fsdp'), may hold values from 1.6041436e-16 to 6.416574e-16
- sq_depth: float32 [9, 3328], P(None, 'fsdp'), may hold values from 1.6041436e-16 to 6.416574e-16
- sq_norms3: float32 [8, 320], P(None, 'fsdp'), may hold values from 1.6041436e-16 to 6.416574e-16
- sq_norms4: float32 [8, 512], P(None, 'fsdp'), may hold values from 1.6041436e-16 to 6.416574e-16
Outputs:
- new_mat3: float32 [320, 2560], P('fsdp')
- new_tall3: float32 [3328, 320], P('fsdp')
- new_mat4: float32 [512, 5096], P('fsdp')
- new_tall4: float32 [3328, 512], P('fsdp')
- new_depth: float32 [9, 3328], P(None, 'fsdp')
- new_norms3: float32 [8, 320], P(None, 'fsdp')
- new_norms4: float32 [8, 512], P(None, 'fsdp')
- first_mat3: float32 [320, 2560], P('fsdp')
- first_tall3: float32 [3328, 320], P('fsdp')
- first_mat4: float32 [512, 5096], P('fsdp')
- first_tall4: float32 [3328, 512], P('fsdp')
- first_depth: float32 [9, 3328], P(None, 'fsdp')
- first_norms3: float32 [8, 320], P(None, 'fsdp')
- first_norms4: float32 [8, 512], P(None, 'fsdp')
- second_mat3: float32 [320, 2560], P('fsdp')
- second_tall3: float32 [3328, 320], P('fsdp')
- second_mat4: float32 [512, 5096], P('fsdp')
- second_tall4: float32 [3328, 512], P('fsdp')
- second_depth: float32 [9, 3328], P(None, 'fsdp')
- second_norms3: float32 [8, 320], P(None, 'fsdp')
- second_norms4: float32 [8, 512], P(None, 'fsdp')
- loss_sum: float32 [], replicated
- image_count: float32 [], replicated
- grad_norm: float32 [], replicated
Inputs may be any that keep to these rules, and one draw needn't show every extreme that they name: `valid`: 1 where the slot holds an image; in every micro-batch the last image slot holds one.
All inputs are finite; a program needn't handle non-finite values.
Results may differ from a plain program's by a relative error of at most 0.0078.
Values may be sent and summed in bfloat16 or wider, within the bound.
No kernel may reach another device: no remote copies, remote signals or barrier semaphores. Data moves between devices by JAX's collectives and lax.ppermute only.
A program may use at most 512 MiB of HBM per device.

v0:
```python
import functools
import math

import jax
import jax.numpy as jnp
from jax import lax
from jax.experimental import pallas as pl
from jax.experimental.pallas import tpu as pltpu
from jax.sharding import PartitionSpec as P

BF = jnp.bfloat16
F32 = jnp.float32
C3 = 320
C3P = 384
H3 = 5
F3 = 1280
C4 = 512
H4 = 8
F4 = 2048
CLASSES = 1000
PATCH = 768
STEP = 10
IMGS = 4
TOK3 = 1024
TOK4 = 256
LC = 256
PART = 8
EPS = 1e-06
SMOOTHING = 0.1
CLIP_LEVEL = 0.001
SCALE = 0.125
LOG2_E = 1.4426950408889634
VMEM_BYTES = 63 * 2**20


def contract(a, b, ca, cb):
    return lax.dot_general(a, b, (((ca,), (cb,)), ((), ())), preferred_element_type=F32)


def nn(a, b):
    return contract(a, b, 1, 0)


def nt(a, b):
    return contract(a, b, 1, 1)


def tn(a, b):
    return contract(a, b, 0, 0)


def normalize(x):
    centred = x - jnp.mean(x, axis=-1, keepdims=True)
    rstd = lax.rsqrt(jnp.mean(centred * centred, axis=-1, keepdims=True) + EPS)
    return centred * rstd, rstd


def norm_grad(dy, xhat, rstd, gain):
    dx = dy * gain
    return rstd * (dx - jnp.mean(dx, axis=-1, keepdims=True) - xhat * jnp.mean(dx * xhat, axis=-1, keepdims=True))


def fold(x, op):
    x = x.reshape(x.shape[0] // 8, 8, x.shape[1])
    while x.shape[0] > 1:
        half = x.shape[0] // 2
        x = op(x[:half], x[half:])
    return x[0]


def column_sum(x):
    return jnp.sum(fold(x, jnp.add), axis=0, keepdims=True)


def half_of(x, half):
    lane = lax.broadcasted_iota(jnp.int32, x.shape, 1)
    keep = (lane < 64) if half == 0 else (lane >= 64)
    return jnp.where(keep, x, jnp.zeros_like(x))


def softmax_rows0(scores):
    top = jnp.max(fold(scores, jnp.maximum), axis=0, keepdims=True)
    exponent = jnp.exp2((scores - top) * (SCALE * LOG2_E))
    return exponent * (1.0 / column_sum(exponent))


def softmax_grad(soft, grad):
    mean = column_sum(grad * soft) / column_sum(soft)
    return soft * (grad - mean)


def gelu_both(c):
    k0 = 0.7978845608028654
    k1 = 0.044715 * k0
    c2 = c * c
    t = jnp.tanh(c * (k1 * c2 + k0))
    half = 0.5 * t + 0.5
    slope = half + c * (half - half * half) * (6.0 * k1 * c2 + 2.0 * k0)
    return c * half, slope


def shift_down(v):
    lane = lax.broadcasted_iota(jnp.int32, v.shape, 1)
    return jnp.where(lane == 0, 0.0, pltpu.roll(v, 1, 1))


def shift_up(v):
    lane = lax.broadcasted_iota(jnp.int32, v.shape, 1)
    return jnp.where(lane == 7, 0.0, pltpu.roll(v, 7, 1))


def class3(py, xm):
    return py * 4 + (xm & 1) * 2 + (xm >> 1)


def store3(plain, moved, plane, value):
    py, px = plane // 2, plane % 2
    value = value.reshape(2, 16, 8, value.shape[-1])
    for qx in range(2):
        plain[plane * 2 + qx, 1:17] = value[qx]
    if px == 1:
        moved[py * 2, 1:17] = shift_down(value[1])
    else:
        moved[py * 2 + 1, 1:17] = shift_up(value[0])


def tap3(plain, moved, py, xm, dy, dx, part, lanes):
    row = (py + dy) % 2
    start = 1 + (py + dy) // 2 + part * PART
    at = xm + dx
    if at == -1:
        return moved[row * 2, start : start + PART, :, lanes]
    if at == 4:
        return moved[row * 2 + 1, start : start + PART, :, lanes]
    return plain[class3(row, at), start : start + PART, :, lanes]


def store4(plain, moved, image, value):
    value = value.reshape(2, 16, 8, value.shape[-1])
    for qx in range(2):
        plain[image, qx, 1:17] = value[qx]
    moved[image, 0, 1:17] = shift_down(value[1])
    moved[image, 1, 1:17] = shift_up(value[0])


def tap4(plain, moved, image, qx, dy, dx, part, lanes):
    start = 1 + dy + part * PART
    at = qx + dx
    if at == -1:
        return moved[image, 0, start : start + PART, :, lanes]
    if at == 2:
        return moved[image, 1, start : start + PART, :, lanes]
    return plain[image, at, start : start + PART, :, lanes]


def up(value, unit):
    return -(-value // unit) * unit


def rows4(shards, groups):
    return up(10 * (C4 // shards) + (4 * C3 + F4) // shards, math.lcm(16, groups))


def places3(shards, groups):
    tall = (PATCH + 4 * C3 + F3) // shards // 2
    mats = up(tall, 16)
    slot = up(C3 // shards, 8)
    flat = up(mats + 4 * slot, 16)
    flat_rows = -(-(9 * (F3 + F4) + 2 * C3 + 8 * C4) // (shards * 2 * C3))
    last = flat + up(flat_rows, 8)
    return mats, slot, flat, flat_rows, last, up(last + 8, 8 * groups)


def piece_copy(out, target, sems, piece, at):
    shard, start, end = piece
    rows = pl.ds(start, end - start)
    return pltpu.make_async_copy(out.at[shard, rows], target.at[shard // 2, rows], sems.at[at])


def send_off(out, keep, send, sems, core, pieces, base):
    for at, piece in enumerate(pieces):

        @pl.when(core == piece[0] % 2)
        def _():
            piece_copy(out, keep, sems, piece, base + at).start()

        @pl.when(core != piece[0] % 2)
        def _():
            piece_copy(out, send, sems, piece, base + at).start()


def arrived(out, keep, sems, pieces, base):
    for at, piece in enumerate(pieces):
        piece_copy(out, keep, sems, piece, base + at).wait()


def store_columns4(out, value, column):
    size = C4 // out.shape[0]
    block, lane = column // C4, column % C4
    start = block * size
    lanes = slice(lane, lane + value.shape[1])
    if not isinstance(column, int):
        start = pl.multiple_of(start, size)
        lanes = pl.ds(pl.multiple_of(lane, LC), value.shape[1])
    for at in range(out.shape[0]):
        out[at, pl.ds(start, size), lanes] = value[at * size : at * size + size].astype(BF)


def store_rows(out, value, row, size, offset):
    at = row
    while at < row + value.shape[0]:
        shard = at // size
        end = min((shard + 1) * size, row + value.shape[0])
        start = offset + at - shard * size
        out[shard, start : start + end - at, :] = value[at - row : end - row].astype(BF)
        at = end


def alternate(many, few):
    done = 0
    for at, one in enumerate(many):
        one()
        while done < len(few) and (done + 1) * len(many) <= (at + 1) * len(few):
            few[done]()
            done += 1


TAPS = [(t, t // 3 - 1, t % 3 - 1) for t in range(9)]


def embed_attend(patches, tall3, mat3, norms, z_o, h_o, red_o, q_o, k_o, v_o, p_o, mix_o, x1_o, x0_s, vt_s):
    def embed(b):
        return nn(patches[0, b * 256 : b * 256 + 256, :], tall3[0:PATCH])

    def project(b, h):
        q_o[0, b * 256 : b * 256 + 256, :] = nn(h, mat3[:, 0:C3P]).astype(BF)
        return nn(h, tall3[PATCH + C3 * b : PATCH + C3 * (b + 1)])

    reduced = None
    later = embed(0)
    for b in range(4):
        rows = pl.ds(b * 256, 256)
        z = later
        if b < 3:
            later = embed(b + 1)
        z_o[0, rows, :] = z
        x0 = normalize(z)[0] * norms[0:1] + norms[1:2]
        x0_s[rows, :] = x0
        h = (normalize(x0)[0] * norms[2:3] + norms[3:4]).astype(BF)
        h_o[0, rows, :] = h
        if b > 0:
            part = project(b - 1, before)
            reduced = part if reduced is None else reduced + part
        before = h
    reduced = reduced + project(3, before)
    red_o[0] = reduced
    r = (normalize(reduced)[0] * norms[4:5] + norms[5:6]).astype(BF)
    k = nn(r, mat3[:, C3P : 2 * C3P]).astype(BF)
    v = nn(r, mat3[:, 2 * C3P : 3 * C3P]).astype(BF)
    k_o[0] = k
    v_o[0] = v
    vt_s[...] = v.T

    def queries():
        rows = [pl.ds(at * 256, 256) for at in range(4)]
        steps = [(rows[at], head) for at in range(4) for head in range(H3)]

        def raw(block, head):
            lanes = slice(head // 2 * 128, head // 2 * 128 + 128)
            return nt(half_of(k_o[0, :, lanes], head % 2), q_o[0, block, lanes])

        def mix(block, head, soft):
            mix_o[0, head * 64 : head * 64 + 64, block] = nn(vt_s[head * 64 : head * 64 + 64, :], soft).astype(BF)
            if head == H3 - 1:
                product = tn(mix_o[0, :, block], mat3[0:C3, 3 * C3P : 3 * C3P + C3])
                x1_o[0, block, :] = x0_s[block, :] + product

        later = raw(*steps[0])
        before = None
        for at, (block, head) in enumerate(steps):
            scores = later
            if at + 1 < len(steps):
                later = raw(*steps[at + 1])
            soft = softmax_rows0(scores).astype(BF)
            p_o[0, head, :, block] = soft
            if at > 0:
                mix(*steps[at - 1], before)
            before = soft
        mix(*steps[-1], before)

    queries()


def feed3(x1, tall3, mat3, depth, norms, n_o, hid_o, slope_o, act_o, x2_o, plain, moved, stage, cur, prev, total):
    @pl.when(pl.program_id(0) == 0)
    def _():
        for ref in (plain, moved):
            ref[:, 0:1] = jnp.zeros((ref.shape[0], 1, 8, LC), F32)
            ref[:, 17:18] = jnp.zeros((ref.shape[0], 1, 8, LC), F32)

    for b in range(4):
        rows = pl.ds(b * 256, 256)
        n_o[0, rows, :] = (normalize(x1[0, rows, :])[0] * norms[6:7] + norms[7:8]).astype(BF)

    chunks = F3 // LC

    def lanes_of(j):
        return pl.ds(pl.multiple_of(j * LC, LC), LC)

    def hidden(j, plane):
        rows = pl.ds(plane * 256, 256)
        stage[rows, :] = nn(n_o[0, rows, :], mat3[:, pl.ds(pl.multiple_of(4 * C3P + j * LC, LC), LC)])

    def spread(j):
        for plane in range(4):
            rows = pl.ds(plane * 256, 256)
            value = stage[rows, :]
            hid_o[0, rows, lanes_of(j)] = value.astype(BF)
            store3(plain, moved, plane, value)

    def second(j, b):
        rows = pl.ds(b * 256, 256)
        return total[rows, :] + nn(prev[rows, :], tall3[pl.ds(pl.multiple_of(PATCH + 4 * C3 + j * LC, LC), LC), :])

    for plane in range(4):
        hidden(0, plane)
    spread(0)
    total[...] = x1[0]
    prev[...] = jnp.zeros_like(prev)

    def chunk(j, carry):
        later = jnp.minimum(j + 1, chunks - 1)
        previous = jnp.maximum(j - 1, 0)
        kernels = [depth[:, pl.ds(pl.multiple_of(j * LC + lt * 128, 128), 128)] for lt in range(LC // 128)]

        def convolve(lt, py, xm, part):
            lanes = pl.ds(lt * 128, 128)
            out_lanes = pl.ds(pl.multiple_of(j * LC + lt * 128, 128), 128)
            out = None
            for t, dy, dx in TAPS:
                term = tap3(plain, moved, py, xm, dy, dx, part, lanes) * kernels[lt][t : t + 1][None]
                out = term if out is None else out + term
            activated, slope = gelu_both(out)
            rows = pl.ds(class3(py, xm) * 128 + part * PART * 8, PART * 8)
            cur[rows, lanes] = activated.reshape(PART * 8, 128).astype(BF)
            slope_o[0, rows, out_lanes] = slope.reshape(PART * 8, 128).astype(BF)

        def accumulate(b):
            total[b * 256 : b * 256 + 256, :] = second(previous, b)

        products = []
        for b in range(4):
            products += [functools.partial(hidden, later, b), functools.partial(accumulate, b)]
        alternate(
            [
                functools.partial(convolve, lt, py, xm, part)
                for lt in range(LC // 128)
                for py in range(2)
                for xm in range(4)
                for part in range(16 // PART)
            ],
            products,
        )
        prev[...] = cur[...]
        act_o[0, :, lanes_of(j)] = cur[...]
        spread(later)
        return carry

    lax.fori_loop(0, chunks, chunk, 0)
    for b in range(4):
        x2_o[0, b * 256 : b * 256 + 256, :] = second(chunks - 1, b).astype(BF)


def section4(
    labels, valid, inv_count, core, x2_h, mat4_h, tall4_h, depth, norms,
    dx2_h, keep, send, gd_o, gn_o, loss_o,
    x2, mat4, tall4, sems, out, first, y1_s, y2_s, h_s, qkv_s, p_s, mix_s, n_s, nt_s, hid_s, slope_s, act_s, plain,
    moved, gd_s, stage, cur, prev,
):
    def load(source, target, at):
        return pltpu.make_async_copy(source, target, sems.at[at])

    loads = [load(tall4_h.at[0 : 4 * C3], tall4.at[0 : 4 * C3], 0)]
    loads += [load(x2_h.at[i], x2.at[i], 1 + i) for i in range(IMGS)]
    loads += [load(mat4_h, mat4, 5), load(tall4_h.at[4 * C3 :], tall4.at[4 * C3 :], 6)]
    for one in loads:
        one.start()
    for ref in (plain, moved):
        for at in (0, 17):
            ref[:, :, at : at + 1] = jnp.zeros((IMGS, 2, 1, 8, LC), F32)

    w1_at = 4 * C4
    wc_at = 4 * C4 + F4
    shards = out.shape[0]
    tall_rows = (4 * C3 + F4) // shards
    tall_at = 10 * (C4 // shards)

    loads[0].wait()
    def downsample(i):
        loads[1 + i].wait()
        prod = None
        for plane in range(4):
            part = nn(x2[i, plane * 256 : plane * 256 + 256, :], tall4[plane * C3 : plane * C3 + C3, :])
            prod = part if prod is None else prod + part
        return prod

    def project(i):
        rows = pl.ds(i * TOK4, TOK4)
        for j in range(3):
            wide = slice(j * C4, j * C4 + C4)
            qkv_s[rows, wide] = nn(h_s[rows, :], mat4[:, wide]).astype(BF)

    later = downsample(0)
    for i in range(IMGS):
        rows = pl.ds(i * TOK4, TOK4)
        prod = later
        if i + 1 < IMGS:
            later = downsample(i + 1)
        first[rows, :] = prod
        y0 = normalize(prod)[0] * norms[0:1] + norms[1:2]
        y1_s[rows, :] = y0
        if i == 1:
            loads[5].wait()
        if i > 0:
            project(i - 1)
        h_s[rows, :] = (normalize(y0)[0] * norms[2:3] + norms[3:4]).astype(BF)
    project(IMGS - 1)

    def attend(pair, carry):
        steps = [(pair * 2 + at, head) for at in range(2) for head in range(H4)]

        def image(i):
            return pl.ds(pl.multiple_of(i * TOK4, TOK4), TOK4)

        def raw(i, head):
            at = head // 2 * 128
            key = half_of(qkv_s[image(i), C4 + at : C4 + at + 128], head % 2)
            return nt(key, qkv_s[image(i), at : at + 128])

        def mix(i, head, soft):
            at = 2 * C4 + head // 2 * 128
            if head % 2 == 0:
                values.append(qkv_s[image(i), at : at + 128].T)
            half = values[-1][head % 2 * 64 : head % 2 * 64 + 64]
            mix_s[head * 64 : head * 64 + 64, image(i)] = nn(half, soft).astype(BF)

        values = []
        later = raw(*steps[0])
        before = None
        for at, (i, head) in enumerate(steps):
            scores = later
            if at + 1 < len(steps):
                later = raw(*steps[at + 1])
            soft = softmax_rows0(scores).astype(BF)
            p_s[i * H4 + head] = soft
            if at > 0:
                mix(*steps[at - 1], before)
            before = soft
        mix(*steps[-1], before)
        return carry

    lax.fori_loop(0, IMGS // 2, attend, 0)

    def output(i):
        return tn(mix_s[:, i * TOK4 : i * TOK4 + TOK4], mat4[:, 3 * C4 : 4 * C4])

    later = output(0)
    for i in range(IMGS):
        rows = pl.ds(i * TOK4, TOK4)
        y1 = y1_s[rows, :] + later
        if i + 1 < IMGS:
            later = output(i + 1)
        y1_s[rows, :] = y1
        y2_s[rows, :] = y1
        n_s[rows, :] = (normalize(y1)[0] * norms[4:5] + norms[5:6]).astype(BF)
    loads[6].wait()

    chunks = F4 // LC
    blocks = [(lt, i, qx, p) for lt in range(LC // 128) for i in range(IMGS) for qx in range(2) for p in range(16 // PART)]

    def lanes_of(j):
        return pl.ds(pl.multiple_of(j * LC, LC), LC)

    def second_rows(j):
        return tall4[pl.ds(pl.multiple_of(4 * C3 + j * LC, LC), LC), :]

    def taps_of(j):
        return [depth[:, pl.ds(pl.multiple_of(j * LC + lt * 128, 128), 128)] for lt in range(LC // 128)]

    def image_rows(i):
        return pl.ds(i * TOK4, TOK4)

    def hidden(j, i):
        stage[image_rows(i), :] = nn(n_s[image_rows(i), :], mat4[:, pl.ds(pl.multiple_of(w1_at + j * LC, LC), LC)])

    def spread(j):
        for i in range(IMGS):
            value = stage[image_rows(i), :]
            hid_s[image_rows(i), lanes_of(j)] = value.astype(BF)
            store4(plain, moved, i, value)

    def accumulate(j, i):
        y2_s[image_rows(i), :] += nn(prev[image_rows(i), :], second_rows(j))

    for i in range(IMGS):
        hidden(0, i)
    spread(0)
    prev[...] = jnp.zeros_like(prev)

    def feed(j, carry):
        later, previous = jnp.minimum(j + 1, chunks - 1), jnp.maximum(j - 1, 0)
        kernels = taps_of(j)

        def convolve(lt, i, qx, part):
            lanes = pl.ds(lt * 128, 128)
            total = None
            for t, dy, dx in TAPS:
                term = tap4(plain, moved, i, qx, dy, dx, part, lanes) * kernels[lt][t : t + 1][None]
                total = term if total is None else total + term
            activated, slope = gelu_both(total)
            rows = pl.ds(i * TOK4 + qx * 128 + part * PART * 8, PART * 8)
            cur[rows, lanes] = activated.reshape(PART * 8, 128).astype(BF)
            out_lanes = pl.ds(pl.multiple_of(j * LC + lt * 128, 128), 128)
            slope_s[rows, out_lanes] = slope.reshape(PART * 8, 128).astype(BF)

        products = []
        for i in range(IMGS):
            products += [functools.partial(hidden, later, i), functools.partial(accumulate, previous, i)]
        alternate([functools.partial(convolve, *block) for block in blocks], products)
        prev[...] = cur[...]
        act_s[:, lanes_of(j)] = cur[...]
        spread(later)
        return carry

    lax.fori_loop(0, chunks, feed, 0)

    pools = []
    hat_means = []
    for i in range(IMGS):
        accumulate(chunks - 1, i)
    for i in range(IMGS):
        hat_mean = jnp.mean(normalize(y2_s[image_rows(i), :])[0], axis=0, keepdims=True)
        hat_means.append(hat_mean)
        pools.append(hat_mean * norms[6:7] + norms[7:8])
    pooled = jnp.concatenate(pools + [jnp.zeros((8 - IMGS, C4), F32)], axis=0).astype(BF)
    logits = nn(pooled, mat4[:, wc_at:])

    row = lax.broadcasted_iota(jnp.int32, (8, CLASSES), 0)
    column = lax.broadcasted_iota(jnp.int32, (8, CLASSES), 1)
    target = jnp.full((8, CLASSES), -1, jnp.int32)
    present = jnp.zeros((8, CLASSES), F32)
    for i in range(IMGS):
        target = jnp.where(row == i, labels[i], target)
        present = jnp.where(row == i, valid[i].astype(F32), present)
    goal = (1.0 - SMOOTHING) * (column == target).astype(F32) + SMOOTHING / CLASSES
    shifted = logits - jnp.max(logits, axis=-1, keepdims=True)
    exponent = jnp.exp(shifted)
    mass = jnp.sum(exponent, axis=-1, keepdims=True)
    log_probs = shifted - jnp.log(mass)
    ce = -jnp.sum(goal * log_probs, axis=-1, keepdims=True)
    loss_o[...] = jnp.broadcast_to(jnp.sum(present[:, 0:1] * ce, axis=0, keepdims=True), (8, 128))
    dlogits = (present * inv_count[0] * (exponent / mass - goal)).astype(BF)

    dclass = tn(pooled, dlogits)
    store_columns4(out, dclass[:, :C4], wc_at)
    store_columns4(out, jnp.concatenate([dclass[:, C4:], jnp.zeros((C4, 2 * C4 - CLASSES), F32)], axis=1), wc_at + C4)
    if tall_at + tall_rows < out.shape[1]:
        out[:, tall_at + tall_rows :, :] = jnp.zeros((shards, out.shape[1] - tall_at - tall_rows, C4), BF)
    dpool = nt(dlogits, mat4[:, wc_at:])
    dgain = None
    for i in range(IMGS):
        rows = pl.ds(i * TOK4, TOK4)
        one = dpool[i : i + 1]
        part = one * hat_means[i]
        dgain = part if dgain is None else dgain + part
        xhat, rstd = normalize(y2_s[rows, :])
        dy2 = norm_grad(jnp.broadcast_to(one * (1.0 / TOK4), (TOK4, C4)), xhat, rstd, norms[6:7])
        y2_s[rows, :] = dy2
    gn_o[6:7] = dgain
    gn_o[7:8] = column_sum(dpool)

    for i in range(IMGS):
        nt_s[:, i * TOK4 : i * TOK4 + TOK4] = n_s[image_rows(i), :].T
        n_s[image_rows(i), :] = y2_s[image_rows(i), :].astype(BF)

    def hidden_grad(j, i):
        stage[image_rows(i), :] = nt(n_s[image_rows(i), :], second_rows(j))

    def spread_grad(j):
        for i in range(IMGS):
            store4(plain, moved, i, stage[image_rows(i), :] * slope_s[image_rows(i), lanes_of(j)].astype(F32))

    def first_grad(j):
        store_columns4(out, nn(nt_s[...], hid_s[:, lanes_of(j)]), w1_at + j * LC)

    for i in range(IMGS):
        hidden_grad(0, i)
    spread_grad(0)

    def feed_back(j, carry):
        later, previous = jnp.minimum(j + 1, chunks - 1), jnp.maximum(j - 1, 0)
        kernels = taps_of(j)
        sums = [[None] * 9 for _ in kernels]

        def convolve(lt, i, qx, part):
            lanes = pl.ds(lt * 128, 128)
            out_lanes = pl.ds(pl.multiple_of(j * LC + lt * 128, 128), 128)
            rows = pl.ds(i * TOK4 + qx * 128 + part * PART * 8, PART * 8)
            base = hid_s[rows, out_lanes].astype(F32).reshape(PART, 8, 128)
            acc = None
            for t, dy, dx in TAPS:
                value = tap4(plain, moved, i, qx, -dy, -dx, part, lanes)
                term = value * kernels[lt][t : t + 1][None]
                acc = term if acc is None else acc + term
                tap_sum = jnp.sum(value * base, axis=0)
                sums[lt][t] = tap_sum if sums[lt][t] is None else sums[lt][t] + tap_sum
            cur[rows, lanes] = acc.reshape(PART * 8, 128).astype(BF)

        def second_grad():
            grad = tn(act_s[:, lanes_of(j)], n_s[...]).astype(BF)
            act_s[0:LC, lanes_of(j)] = grad[:, 0:LC]
            act_s[LC : 2 * LC, lanes_of(j)] = grad[:, LC:]

        products = [second_grad, functools.partial(first_grad, previous)]
        products += [functools.partial(hidden_grad, later, i) for i in range(IMGS)]
        alternate([functools.partial(convolve, *block) for block in blocks], products)
        for lt in range(LC // 128):
            for t in range(9):
                gd_s[t, :, pl.ds(pl.multiple_of(j * LC + lt * 128, 128), 128)] = sums[lt][t]
        hid_s[:, lanes_of(j)] = cur[...]
        spread_grad(later)
        return carry

    lax.fori_loop(0, chunks, feed_back, 0)
    first_grad(chunks - 1)
    for j in range(chunks):
        wide = slice(j * LC, j * LC + LC)
        grad = jnp.concatenate([act_s[0:LC, wide], act_s[LC : 2 * LC, wide]], axis=1)
        store_rows(out, grad, 4 * C3 + j * LC, tall_rows, tall_at)
    for t in range(9):
        gd_o[t : t + 1, :] = column_sum(gd_s[t])

    mats_done, tall_done = 4 * (C4 // shards), up(4 * C3, tall_rows) // tall_rows
    early = [(at, mats_done, tall_at) for at in range(shards)]
    early += [(at, tall_at, out.shape[1]) for at in range(tall_done, shards)]
    send_off(out, keep, send, sems, core[0], early, 8)

    def normed_grad(i):
        return nt(hid_s[image_rows(i), :], mat4[:, w1_at : w1_at + F4])

    dgain = dshift = None
    later = normed_grad(0)
    for i in range(IMGS):
        rows = image_rows(i)
        dn = later
        if i + 1 < IMGS:
            later = normed_grad(i + 1)
        xhat, rstd = normalize(y1_s[rows, :])
        part_g, part_s = column_sum(dn * xhat), column_sum(dn)
        dgain = part_g if dgain is None else dgain + part_g
        dshift = part_s if dshift is None else dshift + part_s
        y2_s[rows, :] = y2_s[rows, :] + norm_grad(dn, xhat, rstd, norms[4:5])
    gn_o[4:5] = dgain
    gn_o[5:6] = dshift

    dprod = y2_s[...].astype(BF)
    store_columns4(out, nn(mix_s[...], dprod), 3 * C4)
    for i in range(IMGS):
        rows = pl.ds(i * TOK4, TOK4)
        n_s[rows, :] = nt(dprod[i * TOK4 : i * TOK4 + TOK4], mat4[:, 3 * C4 : 4 * C4]).astype(BF)

    d_s = slope_s

    def attend_back(pair, carry):
        lane = lax.broadcasted_iota(jnp.int32, (TOK4, 128), 1)
        steps = [(pair * 2 + at, head) for at in range(2) for head in range(H4)]
        dqts, dks, dvs, keys = [], [], [], []

        def image(i):
            return pl.ds(pl.multiple_of(i * TOK4, TOK4), TOK4)

        def at(head):
            return head // 2 * 128

        def first_product(i, head):
            start = 2 * C4 + at(head)
            return nt(half_of(qkv_s[image(i), start : start + 128], head % 2), n_s[image(i), at(head) : at(head) + 128])

        def last_products(i, head, ds):
            dks.append(nn(ds, qkv_s[image(i), at(head) : at(head) + 128]))
            if head % 2 == 0:
                keys.append(qkv_s[image(i), C4 + at(head) : C4 + at(head) + 128].T)
            dqts.append(nn(keys[-1][head % 2 * 64 : head % 2 * 64 + 64], ds))
            if head % 2 == 1:
                start, one = at(head), len(dks) - 1
                dqt = (jnp.concatenate(dqts[-2:], axis=0) * SCALE).astype(BF)
                dk = (jnp.where(lane < 64, dks[one - 1], dks[one]) * SCALE).astype(BF)
                dv = jnp.where(lane < 64, dvs[one - 1], dvs[one]).astype(BF)
                d_s[image(i), start : start + 128] = dqt.T
                d_s[image(i), C4 + start : C4 + start + 128] = dk
                d_s[image(i), 2 * C4 + start : 2 * C4 + start + 128] = dv

        later = first_product(*steps[0])
        before = None
        for step, (i, head) in enumerate(steps):
            dp = later
            if step + 1 < len(steps):
                later = first_product(*steps[step + 1])
            soft = p_s[i * H4 + head]
            dvs.append(nn(soft, n_s[image(i), at(head) : at(head) + 128]))
            ds = softmax_grad(soft.astype(F32), dp).astype(BF)
            if step > 0:
                last_products(*steps[step - 1], before)
            before = ds
        last_products(*steps[-1], before)
        return carry

    lax.fori_loop(0, IMGS // 2, attend_back, 0)
    ht = h_s[...].T
    for j in range(3):
        wide = slice(j * C4, j * C4 + C4)
        store_columns4(out, nn(ht, d_s[:, wide]), j * C4)

    def normed_grad0(i):
        return nt(d_s[image_rows(i), 0 : 3 * C4], mat4[:, 0 : 3 * C4])

    sums = [None] * 4
    later = normed_grad0(0)
    for i in range(IMGS):
        rows = image_rows(i)
        dh = later
        if i + 1 < IMGS:
            later = normed_grad0(i + 1)
        hat0, rstd0 = normalize(first[rows, :])
        hat1, rstd1 = normalize(hat0 * norms[0:1] + norms[1:2])
        dy0 = y2_s[rows, :] + norm_grad(dh, hat1, rstd1, norms[2:3])
        n_s[rows, :] = norm_grad(dy0, hat0, rstd0, norms[0:1]).astype(BF)
        parts = [column_sum(dy0 * hat0), column_sum(dy0), column_sum(dh * hat1), column_sum(dh)]
        sums = [part if old is None else old + part for old, part in zip(sums, parts)]
    gn_o[0:4] = jnp.concatenate(sums, axis=0)
    for plane in range(4):
        total = None
        for i in range(IMGS):
            part = tn(x2[i, plane * 256 : plane * 256 + 256, :], n_s[image_rows(i), :])
            total = part if total is None else total + part
        store_rows(out, total, plane * C3, tall_rows, tall_at)
    late = [(at, 0, mats_done) for at in range(shards)] + [(at, tall_at, out.shape[1]) for at in range(tall_done)]
    send_off(out, keep, send, sems, core[0], late, 8 + len(early))
    stores = [load(x2.at[i], dx2_h.at[i], 1 + i) for i in range(IMGS)]
    for i in range(IMGS):
        for plane in range(4):
            grad = nt(n_s[image_rows(i), :], tall4[plane * C3 : plane * C3 + C3, :])
            x2[i, plane * 256 : plane * 256 + 256, :] = grad.astype(BF)
        stores[i].start()
    for one in stores:
        one.wait()
    arrived(out, keep, sems, early, 8)
    arrived(out, keep, sems, late, 8 + len(early))


def feed3_back(dx2, x1, n, hid, slope, act, tall3, mat3, depth, norms, dx1_o, g1_o, g2_o, gd_o, gn_o,
               acc1, acc2, accd, accn, plain, moved, dy_s, dyt_s, nt_s, da_s, stage, cur):
    step = pl.program_id(0)

    @pl.when(step == 0)
    def _():
        for ref in (plain, moved):
            ref[:, 0:1] = jnp.zeros((ref.shape[0], 1, 8, LC), F32)
            ref[:, 17:18] = jnp.zeros((ref.shape[0], 1, 8, LC), F32)
        for ref in (acc1, acc2, accd, accn):
            ref[...] = jnp.zeros_like(ref)

    dy = dx2[0]
    dy_s[...] = dy
    dyt_s[...] = dy.T
    nt_s[...] = n[0].T

    chunks = F3 // LC

    def lanes_of(j):
        return pl.ds(pl.multiple_of(j * LC, LC), LC)

    def hidden_grad(j, plane):
        rows = pl.ds(plane * 256, 256)
        w2 = tall3[pl.ds(pl.multiple_of(PATCH + 4 * C3 + j * LC, LC), LC), :]
        stage[rows, :] = nt(dy_s[rows, :], w2)

    def spread(j):
        for plane in range(4):
            rows = pl.ds(plane * 256, 256)
            store3(plain, moved, plane, stage[rows, :] * slope[0, rows, lanes_of(j)].astype(F32))

    def first_grad(j):
        acc1[:, lanes_of(j)] += nn(nt_s[...], da_s[:, lanes_of(j)])

    for plane in range(4):
        hidden_grad(0, plane)
    spread(0)

    def chunk(j, carry):
        later = jnp.minimum(j + 1, chunks - 1)
        previous = jnp.where(j > 0, j - 1, chunks)
        kernels, sums = [], []
        for lt in range(LC // 128):
            kernels.append(depth[:, pl.ds(pl.multiple_of(j * LC + lt * 128, 128), 128)])
            sums.append([None] * 9)

        def convolve(lt, py, xm, part):
            lanes = pl.ds(lt * 128, 128)
            out_lanes = pl.ds(pl.multiple_of(j * LC + lt * 128, 128), 128)
            rows = pl.ds(class3(py, xm) * 128 + part * PART * 8, PART * 8)
            base = hid[0, rows, out_lanes].astype(F32).reshape(PART, 8, 128)
            out = None
            for t, dy, dx in TAPS:
                value = tap3(plain, moved, py, xm, -dy, -dx, part, lanes)
                term = value * kernels[lt][t : t + 1][None]
                out = term if out is None else out + term
                tap_sum = jnp.sum(value * base, axis=0)
                sums[lt][t] = tap_sum if sums[lt][t] is None else sums[lt][t] + tap_sum
            cur[rows, lanes] = out.reshape(PART * 8, 128).astype(BF)

        def second_grad():
            acc2[:, lanes_of(j)] += nn(dyt_s[...], act[0, :, lanes_of(j)])

        products = [second_grad, functools.partial(first_grad, previous)]
        products += [functools.partial(hidden_grad, later, plane) for plane in range(4)]
        alternate(
            [
                functools.partial(convolve, lt, py, xm, part)
                for lt in range(LC // 128)
                for py in range(2)
                for xm in range(4)
                for part in range(16 // PART)
            ],
            products,
        )
        for lt in range(LC // 128):
            for t in range(9):
                accd[t, :, pl.ds(pl.multiple_of(j * LC + lt * 128, 128), 128)] += sums[lt][t]
        da_s[:, lanes_of(j)] = cur[...]
        spread(later)
        return carry

    lax.fori_loop(0, chunks, chunk, 0)
    first_grad(chunks - 1)

    def normed_grad(b):
        return nt(da_s[b * 256 : b * 256 + 256, 0:F3], mat3[:, 4 * C3P :])

    later = normed_grad(0)
    for b in range(4):
        rows = pl.ds(b * 256, 256)
        dn = later
        if b < 3:
            later = normed_grad(b + 1)
        xhat, rstd = normalize(x1[0, rows, :])
        accn[0:1] += column_sum(dn * xhat)
        accn[1:2] += column_sum(dn)
        dx1_o[0, rows, :] = dx2[0, rows, :].astype(F32) + norm_grad(dn, xhat, rstd, norms[6:7])

    @pl.when(step == IMGS - 1)
    def _():
        g1_o[...] = acc1[:, 0:F3]
        g2_o[...] = acc2[...].T.astype(g2_o.dtype)
        gn_o[...] = accn[...]
        for t in range(9):
            gd_o[t : t + 1, :] = column_sum(accd[t])


def attend3_back(groups, core, dx1, z, h, red, q, k, v, p, mix, patches, tall3, mat3, norms, g1, g2, flat, keep, send, out, sems,
                 tall_s, acce, accr, accq, acck, accv, acco, accn, dk_s, dv_s, kt_s, dqt_s, dr_s):
    step = pl.program_id(0)

    @pl.when(step == 0)
    def _():
        for ref in (acce, accr, accq, acck, accv, acco, accn):
            ref[...] = jnp.zeros_like(ref)

    kt_s[...] = k[0].T
    dk_s[...] = jnp.zeros_like(dk_s)
    dv_s[...] = jnp.zeros_like(dv_s)
    wo = mat3[0:C3, 3 * C3P : 3 * C3P + C3]
    lane = lax.broadcasted_iota(jnp.int32, (256, 128), 1)

    def queries():
        rows = [pl.ds(at * 256, 256) for at in range(4)]
        lanes = [slice(at * 128, at * 128 + 128) for at in range(3)]
        mixed, dks, dvs = [], [], []
        for block in rows:
            dprod = dx1[0, block, :].astype(BF)
            acco[...] += nn(mix[0, :, block], dprod)
            dmix = nt(dprod, wo).astype(BF)
            mixed.append(jnp.concatenate([dmix, jnp.zeros((256, C3P - C3), BF)], axis=1))
        steps = [(at, head) for at in range(4) for head in range(H3)]

        def first(at, head):
            return nt(half_of(v[0, :, lanes[head // 2]], head % 2), mixed[at][:, lanes[head // 2]])

        def last(at, head, ds):
            dks.append(nn(ds, q[0, rows[at], lanes[head // 2]]))
            dqt = nn(kt_s[head * 64 : head * 64 + 64, :], ds) * SCALE
            dqt_s[head * 64 : head * 64 + 64, rows[at]] = dqt.astype(BF)

        later = first(*steps[0])
        before = None
        for step_at, (at, head) in enumerate(steps):
            dp = later
            if step_at + 1 < len(steps):
                later = first(*steps[step_at + 1])
            soft = p[0, head, :, rows[at]]
            dvs.append(nn(soft, mixed[at][:, lanes[head // 2]]))
            ds = softmax_grad(soft.astype(F32), dp).astype(BF)
            if step_at > 0:
                last(*steps[step_at - 1], before)
            before = ds
        last(*steps[-1], before)
        for at in range(4):
            for pair_at in range(2):
                one = at * H3 + 2 * pair_at
                dk_s[:, lanes[pair_at]] += jnp.where(lane < 64, dks[one], dks[one + 1])
                dv_s[:, lanes[pair_at]] += jnp.where(lane < 64, dvs[one], dvs[one + 1])
            dk_s[:, lanes[2]] += dks[at * H3 + 4]
            dv_s[:, lanes[2]] += dvs[at * H3 + 4]

    queries()

    dk = (dk_s[...] * SCALE).astype(BF)
    dv = dv_s[...].astype(BF)
    hat_r, rstd_r = normalize(red[0])
    r = (hat_r * norms[4:5] + norms[5:6]).astype(BF)
    acck[...] += tn(r, dk)
    accv[...] += tn(r, dv)
    dr = nt(dk, mat3[:, C3P : 2 * C3P]) + nt(dv, mat3[:, 2 * C3P : 3 * C3P])
    accn[4:5] += column_sum(dr * hat_r)
    accn[5:6] += column_sum(dr)
    dred = norm_grad(dr, hat_r, rstd_r, norms[4:5]).astype(BF)
    accq[...] += nn(dqt_s[...], h[0])

    def input_grad(b):
        rows = slice(b * 256, b * 256 + 256)
        wr = tall3[PATCH + C3 * b : PATCH + C3 * (b + 1)]
        return contract(dqt_s[:, rows], mat3[:, 0:C3], 0, 1) + nt(dred, wr)

    def weight_grads(b, dz):
        rows = slice(b * 256, b * 256 + 256)
        accr[C3 * b : C3 * (b + 1)] += tn(h[0, rows, :], dred)
        acce[...] += tn(dz, patches[0, rows, :])

    later = input_grad(0)
    before = None
    for b in range(4):
        rows = pl.ds(b * 256, 256)
        dh = later
        if b < 3:
            later = input_grad(b + 1)
        hat0, rstd0 = normalize(z[0, rows, :])
        hat1, rstd1 = normalize(hat0 * norms[0:1] + norms[1:2])
        accn[2:3] += column_sum(dh * hat1)
        accn[3:4] += column_sum(dh)
        dx0 = dx1[0, rows, :] + norm_grad(dh, hat1, rstd1, norms[2:3])
        accn[0:1] += column_sum(dx0 * hat0)
        accn[1:2] += column_sum(dx0)
        dz = norm_grad(dx0, hat0, rstd0, norms[0:1]).astype(BF)
        if b > 0:
            weight_grads(b - 1, before)
        before = dz
    weight_grads(3, before)

    @pl.when(step == IMGS - 1)
    def _():
        shards = out.shape[0]
        mats, slot, flat_at, flat_rows, last, total_rows = places3(shards, groups)
        mat_rows = C3 // shards
        tall = (PATCH + 4 * C3 + F3) // shards // 2
        out[:, mats:, :] = jnp.zeros((shards, total_rows - mats, 2 * C3), BF)
        if tall < mats:
            out[:, tall:mats, :] = jnp.zeros((shards, mats - tall, 2 * C3), BF)
        tall_s[0:PATCH] = acce[...].T
        tall_s[PATCH : PATCH + 4 * C3] = accr[...]
        tall_s[PATCH + 4 * C3 :] = g2[...].astype(F32)
        accq[...] = accq[...].T
        for at in range(shards):
            rows = slice(at * mat_rows, at * mat_rows + mat_rows)
            pieces = [accq[rows, :], acck[rows, 0:C3], accv[rows, 0:C3], acco[rows, :]]
            start = at * 2 * tall
            pairs = [tall_s[start : start + tall], tall_s[start + tall : start + 2 * tall]]
            out[at, 0:tall, :] = jnp.concatenate(pairs, axis=1).astype(BF)
            for b in range(2):
                pair = jnp.concatenate(pieces[2 * b : 2 * b + 2], axis=1)
                out[at, mats + b * slot : mats + b * slot + mat_rows, :] = pair.astype(BF)
                feed = g1[rows, b * 2 * C3 : b * 2 * C3 + 2 * C3]
                out[at, mats + (b + 2) * slot : mats + (b + 2) * slot + mat_rows, :] = feed.astype(BF)
            out[at, flat_at : flat_at + flat_rows, :] = flat[at]
            out[at, last : last + 6, 0:mat_rows] = accn[:, rows].astype(BF)
        pieces = [(at, 0, total_rows) for at in range(shards)]
        send_off(out, keep, send, sems, core[0], pieces, 0)
        arrived(out, keep, sems, pieces, 0)


def whole(shape, dtype=None):
    return pl.BlockSpec(shape, lambda i: (0,) * len(shape), pipeline_mode=pl.Buffered(1))


def per_image(*shape):
    return pl.BlockSpec((1,) + shape, lambda i: (i,) + (0,) * len(shape))


def sds(*shape, dtype=F32):
    return jax.ShapeDtypeStruct(shape, dtype)


def work(microseconds):
    return pl.CostEstimate(flops=microseconds * 10**9, bytes_accessed=microseconds * 3 * 10**6, transcendentals=0)


PARAMS = pltpu.CompilerParams(vmem_limit_bytes=VMEM_BYTES, dimension_semantics=("arbitrary",))


def unpack3(pack, tall3, mat3):
    half = tall3.shape[0] // pack.shape[0] // 2
    size = C3 // pack.shape[0]
    for at in range(pack.shape[0]):
        start = at * 2 * half
        tall3[start : start + half, :] = pack[at, 0:half, 0:C3]
        tall3[start + half : start + 2 * half, :] = pack[at, 0:half, C3:]
        rows = slice(at * size, at * size + size)
        for b in range(2):
            piece = pack[at, half + b * size : half + (b + 1) * size, :]
            blank = jnp.zeros((size, C3P - C3), BF)
            wide = jnp.concatenate([piece[:, :C3], blank, piece[:, C3:], blank], axis=1)
            mat3[rows, b * 2 * C3P : (b + 1) * 2 * C3P] = wide
            feed = pack[at, half + (b + 2) * size : half + (b + 3) * size, :]
            mat3[rows, 4 * C3P + b * 2 * C3 : 4 * C3P + (b + 1) * 2 * C3] = feed


def forward3(packed, *refs):
    if packed:
        pack, patches, depth, norms, tall3, mat3 = refs[:6]

        @pl.when(pl.program_id(0) == 0)
        def _():
            unpack3(pack, tall3, mat3)

    else:
        tall3, mat3, patches, depth, norms = refs[:5]
    refs = refs[6 if packed else 5 :]
    x1 = refs[8]
    embed_attend(patches, tall3, mat3, norms, *refs[:9], *refs[14:16])
    feed3(x1, tall3, mat3, depth, norms, *refs[9:14], *refs[16:])


def run_forward3(weights, patches, depth, norms3):
    packed = len(weights) == 1
    tall_shape, mat_shape = (PATCH + 4 * C3 + F3, C3), (C3, 4 * C3P + F3)
    full = [whole(tall_shape), whole(mat_shape)] if packed else []
    full_shapes = [sds(*tall_shape, dtype=BF), sds(*mat_shape, dtype=BF)] if packed else []
    weight_specs = [whole(weight.shape) for weight in weights]
    image_specs = [per_image(TOK3, PATCH), whole(depth.shape), whole(norms3.shape)]
    outs = pl.pallas_call(
        functools.partial(forward3, packed),
        grid=(IMGS,),
        in_specs=weight_specs + image_specs,
        out_specs=full + [
            per_image(TOK3, C3), per_image(TOK3, C3), per_image(256, C3), per_image(TOK3, C3P), per_image(256, C3P),
            per_image(256, C3P), per_image(H3, 256, TOK3), per_image(C3, TOK3), per_image(TOK3, C3),
            per_image(TOK3, C3), per_image(TOK3, F3), per_image(TOK3, F3), per_image(TOK3, F3), per_image(TOK3, C3),
        ],
        out_shape=full_shapes + [
            sds(IMGS, TOK3, C3), sds(IMGS, TOK3, C3, dtype=BF), sds(IMGS, 256, C3), sds(IMGS, TOK3, C3P, dtype=BF),
            sds(IMGS, 256, C3P, dtype=BF), sds(IMGS, 256, C3P, dtype=BF), sds(IMGS, H3, 256, TOK3, dtype=BF),
            sds(IMGS, C3, TOK3, dtype=BF), sds(IMGS, TOK3, C3),
            sds(IMGS, TOK3, C3, dtype=BF), sds(IMGS, TOK3, F3, dtype=BF), sds(IMGS, TOK3, F3, dtype=BF),
            sds(IMGS, TOK3, F3, dtype=BF), sds(IMGS, TOK3, C3, dtype=BF),
        ],
        scratch_shapes=[
            pltpu.VMEM((TOK3, C3), F32), pltpu.VMEM((C3P, 256), BF),
            pltpu.VMEM((8, 18, 8, LC), F32), pltpu.VMEM((4, 18, 8, LC), F32), pltpu.VMEM((TOK3, LC), F32),
            pltpu.VMEM((TOK3, LC), BF), pltpu.VMEM((TOK3, LC), BF), pltpu.VMEM((TOK3, C3), F32),
        ],
        compiler_params=PARAMS,
        name="forward3",
        cost_estimate=work(85),
    )(*weights, patches, depth, norms3)
    return outs if packed else [*weights, *outs]


def run_section4(labels, valid, inv_count, core, x2, mat4, tall4, depth, norms4, shards, groups):
    vm = pl.BlockSpec(memory_space=pltpu.VMEM)
    sm = pl.BlockSpec(memory_space=pltpu.SMEM)
    hbm = pl.BlockSpec(memory_space=pl.ANY)
    rows = IMGS * TOK4
    half = sds(shards // 2, rows4(shards, groups), C4, dtype=BF)
    return pl.pallas_call(
        section4,
        in_specs=[sm, sm, sm, sm, hbm, hbm, hbm, vm, vm],
        out_specs=[hbm, hbm, hbm, vm, vm, vm],
        out_shape=[
            sds(IMGS, TOK3, C3, dtype=BF), half, half, sds(9, F4), sds(8, C4),
            sds(8, 128),
        ],
        scratch_shapes=[
            pltpu.VMEM(x2.shape, BF), pltpu.VMEM(mat4.shape, BF), pltpu.VMEM(tall4.shape, BF),
            pltpu.SemaphoreType.DMA((8 + 3 * shards,)), pltpu.VMEM((shards,) + half.shape[1:], BF),
            pltpu.VMEM((rows, C4), F32), pltpu.VMEM((rows, C4), F32), pltpu.VMEM((rows, C4), F32),
            pltpu.VMEM((rows, C4), BF), pltpu.VMEM((rows, 3 * C4), BF), pltpu.VMEM((IMGS * H4, 256, 256), BF),
            pltpu.VMEM((C4, rows), BF), pltpu.VMEM((rows, C4), BF), pltpu.VMEM((C4, rows), BF), pltpu.VMEM((rows, F4), BF),
            pltpu.VMEM((rows, F4), BF), pltpu.VMEM((rows, F4), BF), pltpu.VMEM((IMGS, 2, 18, 8, LC), F32),
            pltpu.VMEM((IMGS, 2, 18, 8, LC), F32), pltpu.VMEM((9, 8, F4), F32),
            pltpu.VMEM((rows, LC), F32), pltpu.VMEM((rows, LC), BF), pltpu.VMEM((rows, LC), BF),
        ],
        compiler_params=pltpu.CompilerParams(vmem_limit_bytes=VMEM_BYTES),
        name="section4",
        cost_estimate=work(90),
    )(labels, valid, inv_count, core, x2, mat4, tall4, depth, norms4)


def run_feed3_back(dx2, x1, n, hid, slope, act, tall3, mat3, depth, norms3):
    return pl.pallas_call(
        feed3_back,
        grid=(IMGS,),
        in_specs=[
            per_image(TOK3, C3), per_image(TOK3, C3), per_image(TOK3, C3), per_image(TOK3, F3), per_image(TOK3, F3),
            per_image(TOK3, F3), whole(tall3.shape), whole(mat3.shape), whole(depth.shape), whole(norms3.shape),
        ],
        out_specs=[per_image(TOK3, C3), whole((C3, F3)), whole((F3, C3)), whole((9, F3)), whole((2, C3))],
        out_shape=[sds(IMGS, TOK3, C3), sds(C3, F3), sds(F3, C3, dtype=BF), sds(9, F3), sds(2, C3)],
        scratch_shapes=[
            pltpu.VMEM((C3, F3 + LC), F32), pltpu.VMEM((C3, F3), F32), pltpu.VMEM((9, 8, F3), F32), pltpu.VMEM((2, C3), F32),
            pltpu.VMEM((8, 18, 8, LC), F32), pltpu.VMEM((4, 18, 8, LC), F32), pltpu.VMEM((TOK3, C3), BF),
            pltpu.VMEM((C3, TOK3), BF), pltpu.VMEM((C3, TOK3), BF), pltpu.VMEM((TOK3, F3 + LC), BF),
            pltpu.VMEM((TOK3, LC), F32), pltpu.VMEM((TOK3, LC), BF),
        ],
        compiler_params=PARAMS,
        name="feed3_back",
        cost_estimate=work(68),
    )(dx2, x1, n, hid, slope, act, tall3, mat3, depth, norms3)


def run_attend3_back(core, dx1, z, h, red, q, k, v, p, mix, patches, tall3, mat3, norms3, g1, g2, flat, groups):
    shards = flat.shape[0]
    total_rows = places3(shards, groups)[-1]
    return pl.pallas_call(
        functools.partial(attend3_back, groups),
        grid=(IMGS,),
        in_specs=[
            pl.BlockSpec(memory_space=pltpu.SMEM),
            per_image(TOK3, C3), per_image(TOK3, C3), per_image(TOK3, C3), per_image(256, C3), per_image(TOK3, C3P),
            per_image(256, C3P), per_image(256, C3P), per_image(H3, 256, TOK3), per_image(C3, TOK3),
            per_image(TOK3, PATCH), whole(tall3.shape), whole(mat3.shape), whole(norms3.shape),
            whole(g1.shape), whole(g2.shape), whole(flat.shape),
        ],
        out_specs=[pl.BlockSpec(memory_space=pl.ANY)] * 2,
        out_shape=[sds(shards // 2, total_rows, 2 * C3, dtype=BF)] * 2,
        scratch_shapes=[
            pltpu.VMEM((shards, total_rows, 2 * C3), BF), pltpu.SemaphoreType.DMA((shards,)),
            pltpu.VMEM((PATCH + 4 * C3 + F3, C3), F32),
            pltpu.VMEM((C3, PATCH), F32), pltpu.VMEM((4 * C3, C3), F32), pltpu.VMEM((C3, C3), F32),
            pltpu.VMEM((C3, C3P), F32), pltpu.VMEM((C3, C3P), F32), pltpu.VMEM((C3, C3), F32), pltpu.VMEM((6, C3), F32),
            pltpu.VMEM((256, C3P), F32), pltpu.VMEM((256, C3P), F32), pltpu.VMEM((C3P, 256), BF),
            pltpu.VMEM((C3, TOK3), BF), pltpu.VMEM((256, C3), F32),
        ],
        compiler_params=PARAMS,
        name="attend3_back",
        cost_estimate=work(65),
    )(core, dx1, z, h, red, q, k, v, p, mix, patches, tall3, mat3, norms3, g1, g2, flat)


def pad_mat3(mat):
    pieces = [mat[:, at * C3 : at * C3 + C3] for at in range(4)]
    pieces = [jnp.pad(piece, ((0, 0), (0, C3P - C3))) for piece in pieces]
    return jnp.concatenate(pieces + [mat[:, 4 * C3 :]], axis=1)


def reorder(patches):
    count = patches.shape[0]
    grid = patches.reshape(count, 16, 2, 8, 2, 2, patches.shape[-1])
    return grid.transpose(0, 2, 5, 4, 1, 3, 6).reshape(patches.shape)


def swap(value, axis, mask):
    return lax.ppermute(value, axis, [(at, at ^ mask) for at in range(lax.axis_size(axis))])


def pick(value, index, axis=0):
    return lax.dynamic_index_in_dim(value, index, axis, keepdims=False)


def add_all(own, parts):
    total = own.astype(F32)
    for part in parts:
        total = total + part.astype(F32)
    return total


def chip_sends(keep, got):
    chip = lax.axis_index("fsdp") // 2
    masks = range(1, keep.shape[0])
    return [add_all(pick(keep, chip ^ mask), [pick(got, chip ^ mask)]).astype(BF) for mask in masks]


def chip_own(keep, got):
    chip = lax.axis_index("fsdp") // 2
    return add_all(pick(keep, chip), [pick(got, chip)])


def depth_sends(shard):
    count, me = lax.axis_size("dp"), lax.axis_index("dp")
    cut = shard.reshape(count, shard.shape[0] // count, shard.shape[1])
    return pick(cut, me), [pick(cut, me ^ mask).astype(BF) for mask in range(1, count)]


def exchange(sends, axis, unit):
    return [swap(send, axis, unit * (at + 1)) for at, send in enumerate(sends)]


def depth_gather(piece):
    count, me = lax.axis_size("dp"), lax.axis_index("dp")
    narrow = piece.astype(BF)
    parts = [narrow] + [swap(narrow, "dp", mask) for mask in range(1, count)]
    placed = [lax.select_n(me, *[parts[at ^ other] for other in range(count)]) for at in range(count)]
    return jnp.concatenate(placed, axis=0).astype(F32)


def total_over_all(row):
    count = lax.axis_size("dp") * lax.axis_size("fsdp")
    rows = jnp.broadcast_to(row, (count, row.shape[1]))
    return jnp.sum(lax.all_to_all(rows, ("dp", "fsdp"), 0, 0, tiled=True), axis=0, keepdims=True)


def adamw(master, moment, second, gradient, is_norm):
    step_rate = 0.5 if is_norm else 0.05
    decay_now = 0.0 if is_norm else 0.05
    first = 0.9 * moment + 0.1 * gradient
    second_new = 0.999 * second + 0.001 * gradient * gradient
    first_hat = first * (1.0 / (1.0 - 0.9**STEP))
    second_hat = second_new * (1.0 / (1.0 - 0.999**STEP))
    updated = master - step_rate * (first_hat / (jnp.sqrt(second_hat) + 1e-08) + decay_now * master)
    return (updated, first, second_new)


def body(patches, labels, valid, *state):
    masters, moments, seconds = state[0:7], state[7:14], state[14:21]
    shards, groups = lax.axis_size("fsdp"), lax.axis_size("dp")
    mat3, tall3, mat4, tall4, depth, norms3, norms4 = [master.astype(BF) for master in masters]
    half, m_rows = tall3.shape[0] // 2, mat3.shape[0]
    pack = [jnp.concatenate([tall3[:half], tall3[half:]], axis=1)]
    pack += [mat3[:, at * 2 * C3 : at * 2 * C3 + 2 * C3] for at in range(4)]
    pack = lax.all_gather(jnp.concatenate(pack, axis=0), "fsdp", axis=0)

    small = [jnp.pad(piece.T, ((0, 0), (0, 16 - piece.shape[0]))) for piece in (depth, norms3, norms4)]
    small.append(jnp.full((8, 16), jnp.sum(valid)).astype(BF))
    sizes = [piece.shape[0] for piece in small]
    small = lax.all_gather(jnp.concatenate(small, axis=0), "fsdp", axis=0)
    edges = [0, sizes[0], sizes[0] + sizes[1], sum(sizes[:3])]
    parts = [small[:, edges[at] : edges[at + 1]].reshape(-1, 16).T.astype(F32) for at in range(3)]
    depth_all, norms3_all, norms4_all = parts[0][:9], parts[1][:8], parts[2][:8]
    present = jnp.full((8, 128), jnp.sum(small[:, edges[3], 0].astype(F32)))
    others = exchange([present] * (groups - 1), "dp", 1)

    weights3 = [pack]
    if half % 8 or m_rows % 8:
        tall3_all = jnp.concatenate([pack[:, :half, :C3], pack[:, :half, C3:]], axis=1).reshape(-1, C3)
        mats = pack[:, half:].reshape(shards, 4, m_rows, 2 * C3).transpose(1, 0, 2, 3).reshape(4, C3, 2 * C3)
        mat3_all = [mats[at // 2, :, at % 2 * C3 : at % 2 * C3 + C3] for at in range(4)]
        mat3_all = [jnp.pad(piece, ((0, 0), (0, C3P - C3))) for piece in mat3_all]
        weights3 = [tall3_all, jnp.concatenate(mat3_all + [mats[2], mats[3]], axis=1)]
    tall4_all = lax.all_gather(tall4, "fsdp", axis=0, tiled=True)
    mat4_all = lax.all_gather(mat4, "fsdp", axis=0, tiled=True)

    patches = reorder(patches.reshape(IMGS, TOK3, PATCH))
    depth3, depth4 = depth_all[:, :F3], depth_all[:, F3:]
    tall3_all, mat3_all, z, h, red, q, k, v, p, mix, x1, n, hid, slope, act, x2 = run_forward3(
        weights3, patches, depth3, norms3_all
    )
    x2, others = lax.optimization_barrier((x2, others))
    image_count = add_all(present, others)[0, 0]
    inv_count = (1.0 / image_count).reshape(1)
    core = (lax.axis_index("fsdp") % 2).reshape(1)
    dx2, keep4, send4, gd4, gn4, loss = run_section4(
        labels.reshape(IMGS), valid.reshape(IMGS), inv_count, core, x2, mat4_all, tall4_all, depth4, norms4_all,
        shards, groups,
    )

    core4 = swap(send4, "fsdp", 1)
    sends4 = chip_sends(keep4, core4)
    dx2, keep4, core4, sends4 = lax.optimization_barrier((dx2, keep4, core4, sends4))
    got4 = exchange(sends4, "fsdp", 2)
    dx1, g1, g2, gd3, gn3b = run_feed3_back(dx2, x1, n, hid, slope, act, tall3_all, mat3_all, depth3, norms3_all)
    dx1, keep4, core4, got4 = lax.optimization_barrier((dx1, keep4, core4, got4))
    own4, sends4 = depth_sends(add_all(chip_own(keep4, core4), got4))

    def by_columns(grad):
        return grad.reshape(grad.shape[0], shards, -1).transpose(1, 0, 2).reshape(shards, -1)

    _, slot, flat_at, flat_rows, last, _ = places3(shards, groups)
    flat = jnp.concatenate([by_columns(grad) for grad in (jnp.concatenate([gd3, gd4], axis=1), gn3b, gn4)], axis=1)
    flat = jnp.pad(flat, ((0, 0), (0, flat_rows * 2 * C3 - flat.shape[1])))
    flat = flat.reshape(shards, flat_rows, 2 * C3).astype(BF)
    dx1, own4, sends4, flat = lax.optimization_barrier((dx1, own4, sends4, flat))
    got4 = exchange(sends4, "dp", 1)
    keep3, send3 = run_attend3_back(
        core, dx1, z, h, red, q, k, v, p, mix, patches, tall3_all, mat3_all, norms3_all, g1, g2, flat, groups
    )
    keep3, send3, got4 = lax.optimization_barrier((keep3, send3, got4))
    piece4 = add_all(own4, got4)
    core3 = swap(send3, "fsdp", 1)
    sends3 = chip_sends(keep3, core3)
    keep3, core3, sends3, piece4 = lax.optimization_barrier((keep3, core3, sends3, piece4))
    got3 = exchange(sends3, "fsdp", 2)
    grads4 = depth_gather(piece4)
    keep3, core3, got3, grads4 = lax.optimization_barrier((keep3, core3, got3, grads4))
    own3, sends3 = depth_sends(add_all(chip_own(keep3, core3), got3))
    piece3 = add_all(own3, exchange(sends3, "dp", 1))
    square = jnp.sum(piece4 * piece4) + jnp.sum(piece3 * piece3)
    lane = lax.broadcasted_iota(jnp.int32, (1, 128), 1)
    totals = total_over_all(jnp.where(lane == 0, square, loss[0:1]))
    grads3 = depth_gather(piece3)

    m_rows, t_rows = C4 // shards, masters[3].shape[0]
    blocks4 = [grads4[at * m_rows : at * m_rows + m_rows] for at in range(10)]
    grad_mat4 = jnp.concatenate(blocks4, axis=1)[:, : masters[2].shape[1]]
    grad_tall4 = grads4[10 * m_rows : 10 * m_rows + t_rows]
    t_rows, m_rows = masters[1].shape[0], masters[0].shape[0]
    mats_at, half = up(t_rows // 2, 16), t_rows // 2
    grad_tall3 = jnp.concatenate([grads3[:half, :C3], grads3[:half, C3:]], axis=0)
    grad_mat3 = jnp.concatenate([grads3[mats_at + at * slot : mats_at + at * slot + m_rows] for at in range(4)], axis=1)
    flat = grads3[flat_at : flat_at + flat_rows].reshape(-1)
    sizes = [9 * t_rows, 2 * m_rows, masters[6].size]
    grad_depth = flat[: sizes[0]].reshape(9, t_rows)
    grad_norms3 = jnp.concatenate(
        [grads3[last : last + 6, :m_rows], flat[sizes[0] : sizes[0] + sizes[1]].reshape(2, m_rows)], axis=0
    )
    grad_norms4 = flat[sizes[0] + sizes[1] : sum(sizes)].reshape(masters[6].shape)
    group = [grad_mat3, grad_tall3, grad_mat4, grad_tall4, grad_depth, grad_norms3, grad_norms4]

    grad_norm = jnp.sqrt(totals[0, 0])
    clip_factor = jnp.minimum(1.0, CLIP_LEVEL / (grad_norm + 1e-06))
    results = [adamw(masters[at], moments[at], seconds[at], clip_factor * group[at], at >= 5) for at in range(7)]
    return (
        *[result[0] for result in results],
        *[result[1] for result in results],
        *[result[2] for result in results],
        totals[0, 1],
        image_count,
        grad_norm,
    )


def solution(mesh):
    rows, columns = P("fsdp", None), P(None, "fsdp")
    weights = (rows,) * 4 + (columns,) * 3
    images = P(None, ("dp", "fsdp"))
    in_specs = (P(None, ("dp", "fsdp"), None, None), images, images) + weights * 3
    out_specs = weights * 3 + (P(), P(), P())
    return jax.shard_map(body, mesh=mesh, in_specs=in_specs, out_specs=out_specs, check_vma=False)
```

profile of v0, /device:TPU:0, one launch (start us, length us, event | category | flops | bytes accessed | tf_op | source)
XLA Modules:
  0.0 434.8 jit_solution(3772743612399115419)
XLA Ops:
  7.2 1.0 convert_element_type.254
  8.3 1.2 convert_element_type.253
  9.7 0.8 copy-done.7
  10.6 0.8 convert_element_type.261
  11.5 0.9 convert_element_type.260
  14.0 11.1 %all-gather.2 = bf16[8,528,16]{1,2,0:T(8,128)(2,1)S(1)} all-gather(bf16[1,528,16]{1,2,0:T(8,128)(2,1)S(1)} %fusion.30), channel_id=2, replica_groups=mesh['dp'=4,'fsdp'=8] {'fsdp'}, dimensions={0}, use_global_device_ids=true | all-gather | bytes 152064 | tf_op jit(solution)/shard_map/all_gather | solution.py:1253
  25.1 0.7 fusion.34
  26.4 3.4 collective-permute-start.2
  29.8 1.1 collective-permute-start
  32.9 13.5 %reshape_reshape.3 = bf16[4,16,2,8,2,2,768]{6,5,4,3,2,1,0:T(2,128)(2,1)} reshape(bf16[4,1,1024,768]{3,2,1,0:T(8,128)(2,1)} %param.24) | data formatting | bytes 12582912 | tf_op jit(solution)/shard_map/reshape;reshape | solution.py:1176
  46.4 6.6 %copy.79 = bf16[4,16,2,8,2,2,768]{6,3,1,4,5,2,0:T(8,128)(2,1)} copy(bf16[4,16,2,8,2,2,768]{6,5,4,3,2,1,0:T(2,128)(2,1)} %reshape_reshape.3) | data formatting | bytes 12582912 | tf_op jit(solution)/shard_map/reshape;reshape | solution.py:1176
  54.2 75.6 %forward3.1 = (bf16[3328,320]{1,0:T(8,128)(2,1)}, bf16[320,2816]{1,0:T(8,128)(2,1)}, f32[4,1024,320]{2,1,0:T(8,128)}, bf16[4,1024,320]{2,1,0:T(8,128)(2,1)}, f32...) custom-call(bf16[8,368,640]{2,1,0:T(8,128)(2,1)} %bitcast.106, ...), custom_call_target="tpu_custom_call" | custom-call | flops 85000003584 | bytes 255000000 | tf_op jit(solution)/shard_map/forward3/pallas_call | solution.py:1059
  131.8 70.8 %section4.1 = (bf16[4,1024,320]{2,1,0:T(8,128)(2,1)}, bf16[4,1056,512]{2,1,0:T(8,128)(2,1)}, bf16[4,1056,512]{2,1,0:T(8,128)(2,1)}, f32[9,2048]{1,0:T(8,128)}, f32[8,512]{1,0:T(8,128)}, /*index=5*/f32[8,128]{1,0:T(8,128)}) custom-call(s32[4]{0:T(128)} %bitcast.107, s32[4]{0:T(128)} %bitcast.108, f32[1]{0:T(128)} %bitcast.13.inv_count, s32[1]{0:T(128)} %bitcast.core, ...), custom_call_target="tpu_custom_call" | custom-call | flops 89999998976 | bytes 270000000 | tf_op jit(solution)/shard_map/section4/pallas_call | solution.py:1093
  202.7 0.7 convert.35
  203.7 0.9 convert.33
  204.6 5.8 %collective-permute-done.3 = bf16[4,1056,512]{2,1,0:T(8,128)(2,1)} collective-permute-done((bf16[4,1056,512]{2,1,0:T(8,128)(2,1)}, bf16[4,1056,512]{2,1,0:T(8,128)(2,1)}, u32[]{:S(2)}, u32[]{:S(2)}) %collective-permute-start.3) | collective-permute-done | bytes 4325408 | tf_op jit(solution)/shard_map/ppermute | solution.py:1181
  210.4 5.1 %fusion.5 = (bf16[1056,512]{1,0:T(8,128)(2,1)}, bf16[1056,512]{1,0:T(8,128)(2,1)}, bf16[1056,512]{1,0:T(8,128)(2,1)}) fusion(bf16[4,1056,512]{2,1,0:T(8,128)(2,1)} %collective-permute-done.3, s32[]{:T(128)S(6)} %select_n.206, bf16[4,1056,512]{2,1,0:T(8,128)(2,1)} %get-tuple-element.115, s32[]{:T(128)S(6)} %select_n.205, s32[]{:T(128)S(6)} %select_n.204), kind=kLoop, calls=%fused_computation.14 | loop fusion | flops 6488064 | bytes 9732108 | tf_op jit(solution)/shard_map/convert_element_type | solution.py:1198
  215.5 1.2 collective-permute-start.4
  216.7 0.9 collective-permute-start.5
  217.5 1.4 collective-permute-start.6
  219.0 64.5 %feed3_back.1 = (f32[4,1024,320]{2,1,0:T(8,128)}, f32[320,1280]{1,0:T(8,128)}, bf16[1280,320]{1,0:T(8,128)(2,1)}, f32[9,1280]{1,0:T(8,128)}, f32[2,320]{1,0:T(2,128)}) custom-call(bf16[4,1024,320]{2,1,0:T(8,128)(2,1)} %get-tuple-element.100.dx2, f32[4,1024,320]{2,1,0:T(8,128)} %get-tuple-element.101.x1, bf16[4,1024,320]{2,1,0:T(8,128)(2,1)} %get-tuple-element.102.n, ...), custom_call_target="tpu_custom_call" | custom-call | flops 67999997952 | bytes 204000000 | tf_op jit(solution)/shard_map/feed3_back/pallas_call | solution.py:1118
  283.5 0.7 convert.34
  284.4 0.9 convert.32
  285.7 3.3 fusion.1
  289.1 0.9 fusion.16
  290.6 1.0 collective-permute-start.7
  291.6 2.9 collective-permute-start.8
  295.0 44.2 %attend3_back.1 = (bf16[4,384,640]{2,1,0:T(8,128)(2,1)}, bf16[4,384,640]{2,1,0:T(8,128)(2,1)}) custom-call(s32[1]{0:T(128)} %bitcast.core, f32[4,1024,320]{2,1,0:T(8,128)} %get-tuple-element.124.dx1, f32[4,1024,320]{2,1,0:T(8,128)} %get-tuple-element.125.z, bf16[4,1024,320]{2,1,0:T(8,128)(2,1)} %get-tuple-element.126.h, ...), custom_call_target="tpu_custom_call" | custom-call | flops 65000001536 | bytes 195000000 | tf_op jit(solution)/shard_map/attend3_back/pallas_call | solution.py:1142
  339.3 1.3 convert_add_fusion
  340.6 2.9 collective-permute-done.10
  343.5 3.2 fusion.12
  346.7 0.7 multiply_reduce_fusion
  347.4 3.3 collective-permute-start.16
  350.7 1.1 collective-permute-start.14
  351.8 1.2 collective-permute-start.11
  353.0 0.9 collective-permute-start.12
  353.9 4.8 %collective-permute-done.16 = bf16[264,512]{1,0:T(8,128)(2,1)S(1)} collective-permute-done((bf16[264,512]{1,0:T(8,128)(2,1)S(1)}, bf16[264,512]{1,0:T(8,128)(2,1)S(1)}, u32[]{:S(2)}, u32[]{:S(2)}) %collective-permute-start.16) | collective-permute-done | bytes 270368 | tf_op jit(solution)/shard_map/ppermute | solution.py:1181
  358.7 1.5 collective-permute-start.13
  360.2 12.7 %collective-permute-done.15 = bf16[264,512]{1,0:T(8,128)(2,1)S(1)} collective-permute-done((bf16[264,512]{1,0:T(8,128)(2,1)S(1)}, bf16[264,512]{1,0:T(8,128)(2,1)S(1)}, u32[]{:S(2)}, u32[]{:S(2)}) %collective-permute-start.15) | collective-permute-done | bytes 270368 | tf_op jit(solution)/shard_map/ppermute | solution.py:1181
  373.3 2.5 collective-permute-done.13
  375.9 1.5 fusion.7
  377.4 5.2 %collective-permute-start.17 = (bf16[96,640]{1,0:T(8,128)(2,1)S(1)}, bf16[96,640]{1,0:T(8,128)(2,1)S(1)}, u32[]{:S(2)}, u32[]{:S(2)}) collective-permute-start(bf16[96,640]{1,0:T(8,128)(2,1)S(1)} %get-tuple-element.198), channel_id=1, source_target_pairs={{0,8},{8,0},{16,24},{24,16},{1,9},{9,1},{17,25},{25,17},{2,10},{10... | collective-permute-start | bytes 368648 | tf_op jit(solution)/shard_map/ppermute | solution.py:1181
  382.6 2.4 collective-permute-start.19
  384.9 0.7 slice_dynamic-update-slice_fusion.9
  385.6 0.7 slice_dynamic-update-slice_fusion.8
  387.0 0.7 slice_dynamic-update-slice_fusion.6
  388.3 0.7 slice_dynamic-update-slice_fusion.4
  390.3 0.7 slice_dynamic-update-slice_fusion.1
  391.0 2.6 collective-permute-done.18
  393.7 1.3 multiply_reduce_fusion.1
  396.3 0.7 fusion.36
  397.6 3.6 all-to-all-start
  401.2 0.7 slice_dynamic-update-slice_fusion
  401.8 3.6 collective-permute-start.22
  405.5 0.8 collective-permute-start.20
  406.2 2.1 all-to-all-done
  409.7 4.8 %multiply_subtract_fusion = (f32[64,5096]{1,0:T(8,128)}, f32[64,5096]{1,0:T(8,128)}, f32[64,5096]{1,0:T(8,128)}) fusion(f32[64,5096]{1,0:T(8,128)S(1)} %copy-done.1, f32[64,5120]{1,0:T(8,128)} %slice_dynamic-update-slice_fusion, f32[]{:T(128)S(6)} %min.3, f32[64,5096]{1,0:T(8,128)} %param.36, f32[64,5096]{1,0:T(8,128)} %param.43), kind=kLoop, calls=%fused_computation.9 | loop fusion | flops 5218304 | bytes 9132036 | tf_op jit(solution)/shard_map/sub | solution.py:1237
  414.6 1.9 multiply_subtract_fusion.1
  416.7 1.1 select_select_fusion.7
  419.1 0.7 maximum_convert_fusion.5
  420.0 0.9 reshape.182
  420.9 0.8 mul.492
  424.0 1.6 multiply_subtract_fusion.2
  425.6 1.2 multiply_subtract_fusion.3
  (159 shorter events, 16.7 us)
Async XLA Ops:
  7.2 47.0 %all-gather.11.cloned.1.call-start = ((), (), s32[]{:S(2)}) async-start(), calls=%async_computation.3 | async-start | bytes 4239360 | tf_op jit(solution)/shard_map/all_gather | solution.py:1248
  8.3 2.3 copy-start.2
  9.6 1.9 copy-start
  9.7 0.8 copy-start.7
  10.5 121.2 %all-gather.9.cloned.1.call-start = ((), (), s32[]{:S(2)}) async-start(), calls=%async_computation.2 | async-start | bytes 3833856 | tf_op jit(solution)/shard_map/all_gather | solution.py:1267
  11.4 1.0 copy-start.30
  11.4 2.3 copy-start.24
  11.4 2.3 copy-start.22
  11.5 2.3 copy-start.18
  11.5 120.3 %all-gather.7.cloned.1.call-start = ((), (), s32[]{:S(2)}) async-start(), calls=%async_computation.1 | async-start | bytes 5898240 | tf_op jit(solution)/shard_map/all_gather | solution.py:1268
  26.4 103.4 %collective-permute-start.2 = (f32[8,128]{1,0:T(8,128)S(1)}, f32[8,128]{1,0:T(8,128)S(1)}, u32[]{:S(2)}, u32[]{:S(2)}) collective-permute-start(f32[8,128]{1,0:T(8,128)S(1)} %broadcast_in_dim.19), channel_id=1, source_target_pairs={{0,24},{8,16},{16,8},{24,0},{1,25},{9,17},{17,9},{25,1},{2,26},{10... | collective-permute-start | bytes 12296 | tf_op jit(solution)/shard_map/ppermute | solution.py:1181
  29.8 100.1 %collective-permute-start.1 = (f32[8,128]{1,0:T(8,128)S(1)}, f32[8,128]{1,0:T(8,128)S(1)}, u32[]{:S(2)}, u32[]{:S(2)}) collective-permute-start(f32[8,128]{1,0:T(8,128)S(1)} %broadcast_in_dim.19), channel_id=1, source_target_pairs={{0,16},{8,24},{16,0},{24,8},{1,17},{9,25},{17,1},{25,9},{2,18},{10... | collective-permute-start | bytes 12296 | tf_op jit(solution)/shard_map/ppermute | solution.py:1181
  29.8 100.1 %collective-permute-start = (f32[8,128]{1,0:T(8,128)S(1)}, f32[8,128]{1,0:T(8,128)S(1)}, u32[]{:S(2)}, u32[]{:S(2)}) collective-permute-start(f32[8,128]{1,0:T(8,128)S(1)} %broadcast_in_dim.19), channel_id=1, source_target_pairs={{0,8},{8,0},{16,24},{24,16},{1,9},{9,1},{17,25},{25,17},{2,10},{10... | collective-permute-start | bytes 12296 | tf_op jit(solution)/shard_map/ppermute | solution.py:1181
  202.6 7.8 %collective-permute-start.3 = (bf16[4,1056,512]{2,1,0:T(8,128)(2,1)}, bf16[4,1056,512]{2,1,0:T(8,128)(2,1)}, u32[]{:S(2)}, u32[]{:S(2)}) collective-permute-start(bf16[4,1056,512]{2,1,0:T(8,128)(2,1)} %get-tuple-element.99), channel_id=1, source_target_pairs={{0,1},{1,0},{2,3},{3,2},{4,5},{5,4},{6,7},{7,6},{8,9},{9,8},{10,11... | collective-permute-start | bytes 12976136 | tf_op jit(solution)/shard_map/ppermute | solution.py:1181
  215.5 70.2 %collective-permute-start.4 = (bf16[1056,512]{1,0:T(8,128)(2,1)}, bf16[1056,512]{1,0:T(8,128)(2,1)}, u32[]{:S(2)}, u32[]{:S(2)}) collective-permute-start(bf16[1056,512]{1,0:T(8,128)(2,1)} %get-tuple-element.111), channel_id=1, source_target_pairs={{0,2},{1,3},{2,0},{3,1},{4,6},{5,7},{6,4},{7,5},{8,10},{9,11},{10,... | collective-permute-start | bytes 3244040 | tf_op jit(solution)/shard_map/ppermute | solution.py:1181
  216.7 69.1 %collective-permute-start.5 = (bf16[1056,512]{1,0:T(8,128)(2,1)}, bf16[1056,512]{1,0:T(8,128)(2,1)}, u32[]{:S(2)}, u32[]{:S(2)}) collective-permute-start(bf16[1056,512]{1,0:T(8,128)(2,1)} %get-tuple-element.112), channel_id=1, source_target_pairs={{0,4},{1,5},{2,6},{3,7},{4,0},{5,1},{6,2},{7,3},{8,12},{9,13},{10,... | collective-permute-start | bytes 3244040 | tf_op jit(solution)/shard_map/ppermute | solution.py:1181
  217.5 68.2 %collective-permute-start.6 = (bf16[1056,512]{1,0:T(8,128)(2,1)}, bf16[1056,512]{1,0:T(8,128)(2,1)}, u32[]{:S(2)}, u32[]{:S(2)}) collective-permute-start(bf16[1056,512]{1,0:T(8,128)(2,1)} %get-tuple-element.113), channel_id=1, source_target_pairs={{0,6},{1,7},{2,4},{3,5},{4,2},{5,3},{6,0},{7,1},{8,14},{9,15},{10,... | collective-permute-start | bytes 3244040 | tf_op jit(solution)/shard_map/ppermute | solution.py:1181
  290.6 48.6 %collective-permute-start.7 = (bf16[264,512]{1,0:T(8,128)(2,1)}, bf16[264,512]{1,0:T(8,128)(2,1)}, u32[]{:S(2)}, u32[]{:S(2)}) collective-permute-start(bf16[264,512]{1,0:T(8,128)(2,1)} %get-tuple-element.138), channel_id=1, source_target_pairs={{0,8},{8,0},{16,24},{24,16},{1,9},{9,1},{17,25},{25,17},{2,10},{10... | collective-permute-start | bytes 811016 | tf_op jit(solution)/shard_map/ppermute | solution.py:1181
  291.6 47.6 %collective-permute-start.8 = (bf16[264,512]{1,0:T(8,128)(2,1)}, bf16[264,512]{1,0:T(8,128)(2,1)}, u32[]{:S(2)}, u32[]{:S(2)}) collective-permute-start(bf16[264,512]{1,0:T(8,128)(2,1)} %get-tuple-element.139), channel_id=1, source_target_pairs={{0,16},{8,24},{16,0},{24,8},{1,17},{9,25},{17,1},{25,9},{2,18},{10... | collective-permute-start | bytes 811016 | tf_op jit(solution)/shard_map/ppermute | solution.py:1181
  294.5 44.7 %collective-permute-start.9 = (bf16[264,512]{1,0:T(8,128)(2,1)S(1)}, bf16[264,512]{1,0:T(8,128)(2,1)}, u32[]{:S(2)}, u32[]{:S(2)}) collective-permute-start(bf16[264,512]{1,0:T(8,128)(2,1)S(1)} %get-tuple-element.140), channel_id=1, source_target_pairs={{0,24},{8,16},{16,8},{24,0},{1,25},{9,17},{17,9},{25,1},{2,26},{10... | collective-permute-start | bytes 811016 | tf_op jit(solution)/shard_map/ppermute | solution.py:1181
  339.2 4.2 collective-permute-start.10
  343.5 3.2 copy-start.5
  347.4 11.3 %collective-permute-start.16 = (bf16[264,512]{1,0:T(8,128)(2,1)S(1)}, bf16[264,512]{1,0:T(8,128)(2,1)S(1)}, u32[]{:S(2)}, u32[]{:S(2)}) collective-permute-start(bf16[264,512]{1,0:T(8,128)(2,1)S(1)} %get-tuple-element.202), channel_id=1, source_target_pairs={{0,24},{8,16},{16,8},{24,0},{1,25},{9,17},{17,9},{25,1},{2,26},{10... | collective-permute-start | bytes 811016 | tf_op jit(solution)/shard_map/ppermute | solution.py:1181
  350.7 22.1 %collective-permute-start.15 = (bf16[264,512]{1,0:T(8,128)(2,1)S(1)}, bf16[264,512]{1,0:T(8,128)(2,1)S(1)}, u32[]{:S(2)}, u32[]{:S(2)}) collective-permute-start(bf16[264,512]{1,0:T(8,128)(2,1)S(1)} %get-tuple-element.202), channel_id=1, source_target_pairs={{0,16},{8,24},{16,0},{24,8},{1,17},{9,25},{17,1},{25,9},{2,18},{10... | collective-permute-start | bytes 811016 | tf_op jit(solution)/shard_map/ppermute | solution.py:1181
  350.7 22.1 %collective-permute-start.14 = (bf16[264,512]{1,0:T(8,128)(2,1)S(1)}, bf16[264,512]{1,0:T(8,128)(2,1)S(1)}, u32[]{:S(2)}, u32[]{:S(2)}) collective-permute-start(bf16[264,512]{1,0:T(8,128)(2,1)S(1)} %get-tuple-element.202), channel_id=1, source_target_pairs={{0,8},{8,0},{16,24},{24,16},{1,9},{9,1},{17,25},{25,17},{2,10},{10... | collective-permute-start | bytes 811016 | tf_op jit(solution)/shard_map/ppermute | solution.py:1181
  351.8 21.5 %collective-permute-start.11 = (bf16[384,640]{1,0:T(8,128)(2,1)}, bf16[384,640]{1,0:T(8,128)(2,1)S(1)}, u32[]{:S(2)}, u32[]{:S(2)}) collective-permute-start(bf16[384,640]{1,0:T(8,128)(2,1)} %get-tuple-element.150), channel_id=1, source_target_pairs={{0,2},{1,3},{2,0},{3,1},{4,6},{5,7},{6,4},{7,5},{8,10},{9,11},{10,... | collective-permute-start | bytes 1474568 | tf_op jit(solution)/shard_map/ppermute | solution.py:1181
  353.0 20.3 %collective-permute-start.12 = (bf16[384,640]{1,0:T(8,128)(2,1)S(1)}, bf16[384,640]{1,0:T(8,128)(2,1)S(1)}, u32[]{:S(2)}, u32[]{:S(2)}) collective-permute-start(bf16[384,640]{1,0:T(8,128)(2,1)S(1)} %get-tuple-element.151), channel_id=1, source_target_pairs={{0,4},{1,5},{2,6},{3,7},{4,0},{5,1},{6,2},{7,3},{8,12},{9,13},{10,... | collective-permute-start | bytes 1474568 | tf_op jit(solution)/shard_map/ppermute | solution.py:1181
  358.7 17.2 %collective-permute-start.13 = (bf16[384,640]{1,0:T(8,128)(2,1)S(1)}, bf16[384,640]{1,0:T(8,128)(2,1)S(1)}, u32[]{:S(2)}, u32[]{:S(2)}) collective-permute-start(bf16[384,640]{1,0:T(8,128)(2,1)S(1)} %get-tuple-element.152), channel_id=1, source_target_pairs={{0,6},{1,7},{2,4},{3,5},{4,2},{5,3},{6,0},{7,1},{8,14},{9,15},{10,... | collective-permute-start | bytes 1474568 | tf_op jit(solution)/shard_map/ppermute | solution.py:1181
  377.4 13.6 %collective-permute-start.17 = (bf16[96,640]{1,0:T(8,128)(2,1)S(1)}, bf16[96,640]{1,0:T(8,128)(2,1)S(1)}, u32[]{:S(2)}, u32[]{:S(2)}) collective-permute-start(bf16[96,640]{1,0:T(8,128)(2,1)S(1)} %get-tuple-element.198), channel_id=1, source_target_pairs={{0,8},{8,0},{16,24},{24,16},{1,9},{9,1},{17,25},{25,17},{2,10},{10... | collective-permute-start | bytes 368648 | tf_op jit(solution)/shard_map/ppermute | solution.py:1181
  382.6 8.4 %collective-permute-start.19 = (bf16[96,640]{1,0:T(8,128)(2,1)S(1)}, bf16[96,640]{1,0:T(8,128)(2,1)S(1)}, u32[]{:S(2)}, u32[]{:S(2)}) collective-permute-start(bf16[96,640]{1,0:T(8,128)(2,1)S(1)} %get-tuple-element.199), channel_id=1, source_target_pairs={{0,24},{8,16},{16,8},{24,0},{1,25},{9,17},{17,9},{25,1},{2,26},{10... | collective-permute-start | bytes 368648 | tf_op jit(solution)/shard_map/ppermute | solution.py:1181
  384.9 8.7 %collective-permute-start.18 = (bf16[96,640]{1,0:T(8,128)(2,1)S(1)}, bf16[96,640]{1,0:T(8,128)(2,1)S(1)}, u32[]{:S(2)}, u32[]{:S(2)}) collective-permute-start(bf16[96,640]{1,0:T(8,128)(2,1)S(1)} %get-tuple-element.200), channel_id=1, source_target_pairs={{0,16},{8,24},{16,0},{24,8},{1,17},{9,25},{17,1},{25,9},{2,18},{10... | collective-permute-start | bytes 368648 | tf_op jit(solution)/shard_map/ppermute | solution.py:1181
  387.0 22.7 %copy-start.1 = (f32[64,5096]{1,0:T(8,128)S(1)}, f32[64,5096]{1,0:T(8,128)}, u32[]{:S(2)}) copy-start(f32[64,5096]{1,0:T(8,128)} %param.29) | copy-start | bytes 3913732
  397.6 10.7 %all-to-all-start = ((f32[32,1,128]{2,1,0:T(1,128)}), f32[32,1,128]{2,1,0:T(1,128)S(1)}, u32[]{:S(2)}, u32[]{:S(2)}) async-start(f32[32,1,128]{2,1,0:T(1,128)} %broadcast_in_dim.21), calls=%async_computation | async-start | bytes 32768 | tf_op jit(solution)/shard_map/all_to_all | solution.py:1227
  401.8 14.7 %collective-permute-start.22 = (bf16[96,640]{1,0:T(8,128)(2,1)}, bf16[96,640]{1,0:T(8,128)(2,1)}, u32[]{:S(2)}, u32[]{:S(2)}) collective-permute-start(bf16[96,640]{1,0:T(8,128)(2,1)} %get-tuple-element.191), channel_id=1, source_target_pairs={{0,24},{8,16},{16,8},{24,0},{1,25},{9,17},{17,9},{25,1},{2,26},{10... | collective-permute-start | bytes 368648 | tf_op jit(solution)/shard_map/ppermute | solution.py:1181
  405.5 11.3 %collective-permute-start.21 = (bf16[96,640]{1,0:T(8,128)(2,1)}, bf16[96,640]{1,0:T(8,128)(2,1)}, u32[]{:S(2)}, u32[]{:S(2)}) collective-permute-start(bf16[96,640]{1,0:T(8,128)(2,1)} %get-tuple-element.191), channel_id=1, source_target_pairs={{0,16},{8,24},{16,0},{24,8},{1,17},{9,25},{17,1},{25,9},{2,18},{10... | collective-permute-start | bytes 368648 | tf_op jit(solution)/shard_map/ppermute | solution.py:1181
  405.5 11.3 %collective-permute-start.20 = (bf16[96,640]{1,0:T(8,128)(2,1)}, bf16[96,640]{1,0:T(8,128)(2,1)}, u32[]{:S(2)}, u32[]{:S(2)}) collective-permute-start(bf16[96,640]{1,0:T(8,128)(2,1)} %get-tuple-element.191), channel_id=1, source_target_pairs={{0,8},{8,0},{16,24},{24,16},{1,9},{9,1},{17,25},{25,17},{2,10},{10... | collective-permute-start | bytes 368648 | tf_op jit(solution)/shard_map/ppermute | solution.py:1181
  409.7 4.9 %copy-start.3 = (f32[416,512]{1,0:T(8,128)S(1)}, f32[416,512]{1,0:T(8,128)}, u32[]{:S(2)}) copy-start(f32[416,512]{1,0:T(8,128)} %param.30) | copy-start | bytes 2555908
  409.7 4.9 %copy-start.8 = (f32[416,512]{1,0:T(8,128)S(1)}, f32[416,512]{1,0:T(8,128)}, u32[]{:S(2)}) copy-start(f32[416,512]{1,0:T(8,128)} %param.37) | copy-start | bytes 2555908
  409.7 4.9 %copy-start.9 = (f32[416,512]{1,0:T(8,128)S(1)}, f32[416,512]{1,0:T(8,128)}, u32[]{:S(2)}) copy-start(f32[416,512]{1,0:T(8,128)} %param.44) | copy-start | bytes 2555908
  414.6 2.2 copy-start.12
  419.8 2.1 copy-start.23
  419.8 2.7 copy-start.19
  419.8 3.4 copy-start.25
  419.8 4.0 copy-start.4
  419.8 4.0 copy-start.10
  419.9 4.0 copy-start.11
  419.9 2.0 copy-start.26
  420.0 2.0 copy-start.27
  420.0 2.6 copy-start.20
  420.0 2.6 copy-start.21
  420.0 3.2 copy-start.28
  420.0 3.2 copy-start.29
  423.9 1.6 copy-start.6
  423.9 1.6 copy-start.13
  423.9 1.6 copy-start.14
  423.9 1.6 copy-start.15
  423.9 1.6 copy-start.16
  423.9 1.7 copy-start.17
Sparse Core Ops, SparseCore 0:
  10.6 37.7 all-gather.10
  50.9 33.4 all-gather.8
  86.8 41.1 all-gather.6
where the time goes:
time: 438 us; the launch traced here: 435 us
  Pallas kernels  255 us (58%)
  other arithmetic  42.1 us (10%)
  local copies, waits for them, and re-layouts  37.3 us (9%)
  starting transfers between devices  36 us (8%)
  waiting for transfers between devices  33.8 us (8%)
  between operations  19.4 us (4%)
  blocking collectives  11.1 us (3%)
    pallas_call x1, Pallas kernels, run_forward3(): pl.pallas_call(functools.partial(forward3, packed), grid=(IMGS,), in_spec...  75.6 us
    pallas_call x1, Pallas kernels, run_section4(): pl.pallas_call(section4, in_specs=[sm, sm, sm, sm, hbm, hbm, hbm, vm, vm]...  70.8 us
    pallas_call x1, Pallas kernels, run_feed3_back(): pl.pallas_call(feed3_back, grid=(IMGS,), in_specs=[per_image(TOK3, C3), p...  64.5 us
    pallas_call x1, Pallas kernels, run_attend3_back(): pl.pallas_call(functools.partial(attend3_back, groups), grid=(IMGS,), in_...  44.2 us
    ppermute x23, starting transfers between devices, swap(): lax.ppermute(value, axis, [(at, at ^ mask) for at in range(lax.axis_size(...  32.4 us
    ppermute x23, waiting for transfers between devices, swap(): lax.ppermute(value, axis, [(at, at ^ mask) for at in range(lax.axis_size(...  31.6 us
    another operation x2, local copies, waits for them, and re-layouts, reorder(): grid = patches.reshape(count, 16, 2, 8, 2, 2, patches.shape[-1])  20 us
    sub x7, other arithmetic, adamw(): master - step_rate * (first_hat / (jnp.sqrt(second_hat) + 1e-08) + decay_...  11.5 us
  transfers between devices with their start and end apart: 27, of which 8 were waited for; matrix products, arithmetic and copies ran while one was open for 11% of the time, Pallas kernels for 42%

commit v1 on v0

--- a/solution.py
+++ b/solution.py
@@ -427,7 +427,7 @@
     project(IMGS - 1)
 
     def attend(pair, carry):
-        steps = [(pair * 2 + at, head) for at in range(2) for head in range(H4)]
+        steps = [(pair * IMGS + at, head) for at in range(IMGS) for head in range(H4)]
 
         def image(i):
             return pl.ds(pl.multiple_of(i * TOK4, TOK4), TOK4)
@@ -459,7 +459,7 @@
         mix(*steps[-1], before)
         return carry
 
-    lax.fori_loop(0, IMGS // 2, attend, 0)
+    lax.fori_loop(0, 1, attend, 0)
 
     def output(i):
         return tn(mix_s[:, i * TOK4 : i * TOK4 + TOK4], mat4[:, 3 * C4 : 4 * C4])
@@ -673,7 +673,7 @@
 
     def attend_back(pair, carry):
         lane = lax.broadcasted_iota(jnp.int32, (TOK4, 128), 1)
-        steps = [(pair * 2 + at, head) for at in range(2) for head in range(H4)]
+        steps = [(pair * IMGS + at, head) for at in range(IMGS) for head in range(H4)]
         dqts, dks, dvs, keys = [], [], [], []
 
         def image(i):
@@ -715,7 +715,7 @@
         last_products(*steps[-1], before)
         return carry
 
-    lax.fori_loop(0, IMGS // 2, attend_back, 0)
+    lax.fori_loop(0, 1, attend_back, 0)
     ht = h_s[...].T
     for j in range(3):
         wide = slice(j * C4, j * C4 + C4)

time: 438 us -> 437 us (level)
  transfers between devices with their start and end apart: 27 -> 27, of which waited for: 8 -> 8; matrix products, arithmetic and copies ran while one was open for 11% -> 11% of each run, Pallas kernels for 42% -> 43%
where the time goes in v1:
time: 437 us; the launch traced here: 434 us
  Pallas kernels  254 us (58%)
  other arithmetic  42 us (10%)
  local copies, waits for them, and re-layouts  37.4 us (9%)
  starting transfers between devices  36 us (8%)
  waiting for transfers between devices  33.9 us (8%)
  between operations  19.3 us (4%)
  blocking collectives  11.1 us (3%)
    pallas_call x1, Pallas kernels, run_forward3(): pl.pallas_call(functools.partial(forward3, packed), grid=(IMGS,), in_spec...  76 us
    pallas_call x1, Pallas kernels, run_section4(): pl.pallas_call(section4, in_specs=[sm, sm, sm, sm, hbm, hbm, hbm, vm, vm]...  69.2 us
    pallas_call x1, Pallas kernels, run_feed3_back(): pl.pallas_call(feed3_back, grid=(IMGS,), in_specs=[per_image(TOK3, C3), p...  64.7 us
    pallas_call x1, Pallas kernels, run_attend3_back(): pl.pallas_call(functools.partial(attend3_back, groups), grid=(IMGS,), in_...  44.1 us
    ppermute x23, starting transfers between devices, swap(): lax.ppermute(value, axis, [(at, at ^ mask) for at in range(lax.axis_size(...  32.3 us
    ppermute x23, waiting for transfers between devices, swap(): lax.ppermute(value, axis, [(at, at ^ mask) for at in range(lax.axis_size(...  31.7 us
    another operation x2, local copies, waits for them, and re-layouts, reorder(): grid = patches.reshape(count, 16, 2, 8, 2, 2, patches.shape[-1])  20.2 us
    sub x7, other arithmetic, adamw(): master - step_rate * (first_hat / (jnp.sqrt(second_hat) + 1e-08) + decay_...  11.5 us
  transfers between devices with their start and end apart: 27, of which 8 were waited for; matrix products, arithmetic and copies ran while one was open for 11% of the time, Pallas kernels for 43%

profile of v1, /device:TPU:0, one launch (start us, length us, event | category | flops | bytes accessed | tf_op | source)
XLA Modules:
  0.0 433.7 jit_solution(2175967304877698866)
XLA Ops:
  7.2 1.0 convert_element_type.254
  8.3 1.2 convert_element_type.253
  9.7 0.8 copy-done.7
  10.6 0.8 convert_element_type.261
  11.5 0.9 convert_element_type.260
  14.0 11.1 %all-gather.2 = bf16[8,528,16]{1,2,0:T(8,128)(2,1)S(1)} all-gather(bf16[1,528,16]{1,2,0:T(8,128)(2,1)S(1)} %fusion.30), channel_id=2, replica_groups=mesh['dp'=4,'fsdp'=8] {'fsdp'}, dimensions={0}, use_global_device_ids=true | all-gather | bytes 152064 | tf_op jit(solution)/shard_map/all_gather | solution.py:1253
  25.1 0.7 fusion.34
  26.4 3.4 collective-permute-start.2
  29.8 1.1 collective-permute-start
  32.9 13.6 %reshape_reshape.3 = bf16[4,16,2,8,2,2,768]{6,5,4,3,2,1,0:T(2,128)(2,1)} reshape(bf16[4,1,1024,768]{3,2,1,0:T(8,128)(2,1)} %param.24) | data formatting | bytes 12582912 | tf_op jit(solution)/shard_map/reshape;reshape | solution.py:1176
  46.5 6.6 %copy.79 = bf16[4,16,2,8,2,2,768]{6,3,1,4,5,2,0:T(8,128)(2,1)} copy(bf16[4,16,2,8,2,2,768]{6,5,4,3,2,1,0:T(2,128)(2,1)} %reshape_reshape.3) | data formatting | bytes 12582912 | tf_op jit(solution)/shard_map/reshape;reshape | solution.py:1176
  54.3 76.0 %forward3.1 = (bf16[3328,320]{1,0:T(8,128)(2,1)}, bf16[320,2816]{1,0:T(8,128)(2,1)}, f32[4,1024,320]{2,1,0:T(8,128)}, bf16[4,1024,320]{2,1,0:T(8,128)(2,1)}, f32...) custom-call(bf16[8,368,640]{2,1,0:T(8,128)(2,1)} %bitcast.106, ...), custom_call_target="tpu_custom_call" | custom-call | flops 85000003584 | bytes 255000000 | tf_op jit(solution)/shard_map/forward3/pallas_call | solution.py:1059
  132.2 69.2 %section4.1 = (bf16[4,1024,320]{2,1,0:T(8,128)(2,1)}, bf16[4,1056,512]{2,1,0:T(8,128)(2,1)}, bf16[4,1056,512]{2,1,0:T(8,128)(2,1)}, f32[9,2048]{1,0:T(8,128)}, f32[8,512]{1,0:T(8,128)}, /*index=5*/f32[8,128]{1,0:T(8,128)}) custom-call(s32[4]{0:T(128)} %bitcast.107, s32[4]{0:T(128)} %bitcast.108, f32[1]{0:T(128)} %bitcast.13.inv_count, s32[1]{0:T(128)} %bitcast.core, ...), custom_call_target="tpu_custom_call" | custom-call | flops 89999998976 | bytes 270000000 | tf_op jit(solution)/shard_map/section4/pallas_call | solution.py:1093
  201.6 0.7 convert.35
  202.5 0.9 convert.33
  203.5 5.8 %collective-permute-done.3 = bf16[4,1056,512]{2,1,0:T(8,128)(2,1)} collective-permute-done((bf16[4,1056,512]{2,1,0:T(8,128)(2,1)}, bf16[4,1056,512]{2,1,0:T(8,128)(2,1)}, u32[]{:S(2)}, u32[]{:S(2)}) %collective-permute-start.3) | collective-permute-done | bytes 4325408 | tf_op jit(solution)/shard_map/ppermute | solution.py:1181
  209.2 5.1 %fusion.5 = (bf16[1056,512]{1,0:T(8,128)(2,1)}, bf16[1056,512]{1,0:T(8,128)(2,1)}, bf16[1056,512]{1,0:T(8,128)(2,1)}) fusion(bf16[4,1056,512]{2,1,0:T(8,128)(2,1)} %collective-permute-done.3, s32[]{:T(128)S(6)} %select_n.206, bf16[4,1056,512]{2,1,0:T(8,128)(2,1)} %get-tuple-element.115, s32[]{:T(128)S(6)} %select_n.205, s32[]{:T(128)S(6)} %select_n.204), kind=kLoop, calls=%fused_computation.14 | loop fusion | flops 6488064 | bytes 9732108 | tf_op jit(solution)/shard_map/convert_element_type | solution.py:1198
  214.4 1.1 collective-permute-start.4
  215.5 0.9 collective-permute-start.5
  216.4 1.4 collective-permute-start.6
  217.8 64.7 %feed3_back.1 = (f32[4,1024,320]{2,1,0:T(8,128)}, f32[320,1280]{1,0:T(8,128)}, bf16[1280,320]{1,0:T(8,128)(2,1)}, f32[9,1280]{1,0:T(8,128)}, f32[2,320]{1,0:T(2,128)}) custom-call(bf16[4,1024,320]{2,1,0:T(8,128)(2,1)} %get-tuple-element.100.dx2, f32[4,1024,320]{2,1,0:T(8,128)} %get-tuple-element.101.x1, bf16[4,1024,320]{2,1,0:T(8,128)(2,1)} %get-tuple-element.102.n, ...), custom_call_target="tpu_custom_call" | custom-call | flops 67999997952 | bytes 204000000 | tf_op jit(solution)/shard_map/feed3_back/pallas_call | solution.py:1118
  282.5 0.7 convert.34
  283.4 0.9 convert.32
  284.8 3.3 fusion.1
  288.1 0.9 fusion.16
  289.7 1.0 collective-permute-start.7
  290.7 2.8 collective-permute-start.8
  294.1 44.1 %attend3_back.1 = (bf16[4,384,640]{2,1,0:T(8,128)(2,1)}, bf16[4,384,640]{2,1,0:T(8,128)(2,1)}) custom-call(s32[1]{0:T(128)} %bitcast.core, f32[4,1024,320]{2,1,0:T(8,128)} %get-tuple-element.124.dx1, f32[4,1024,320]{2,1,0:T(8,128)} %get-tuple-element.125.z, bf16[4,1024,320]{2,1,0:T(8,128)(2,1)} %get-tuple-element.126.h, ...), custom_call_target="tpu_custom_call" | custom-call | flops 65000001536 | bytes 195000000 | tf_op jit(solution)/shard_map/attend3_back/pallas_call | solution.py:1142
  338.3 1.3 convert_add_fusion
  339.5 2.9 collective-permute-done.10
  342.5 3.2 fusion.12
  345.6 0.7 multiply_reduce_fusion
  346.4 3.3 collective-permute-start.16
  349.7 1.1 collective-permute-start.14
  350.8 1.1 collective-permute-start.11
  351.9 0.9 collective-permute-start.12
  352.8 4.8 %collective-permute-done.16 = bf16[264,512]{1,0:T(8,128)(2,1)S(1)} collective-permute-done((bf16[264,512]{1,0:T(8,128)(2,1)S(1)}, bf16[264,512]{1,0:T(8,128)(2,1)S(1)}, u32[]{:S(2)}, u32[]{:S(2)}) %collective-permute-start.16) | collective-permute-done | bytes 270368 | tf_op jit(solution)/shard_map/ppermute | solution.py:1181
  357.6 1.5 collective-permute-start.13
  359.1 12.7 %collective-permute-done.15 = bf16[264,512]{1,0:T(8,128)(2,1)S(1)} collective-permute-done((bf16[264,512]{1,0:T(8,128)(2,1)S(1)}, bf16[264,512]{1,0:T(8,128)(2,1)S(1)}, u32[]{:S(2)}, u32[]{:S(2)}) %collective-permute-start.15) | collective-permute-done | bytes 270368 | tf_op jit(solution)/shard_map/ppermute | solution.py:1181
  372.3 2.5 collective-permute-done.13
  374.8 1.5 fusion.7
  376.4 5.2 %collective-permute-start.17 = (bf16[96,640]{1,0:T(8,128)(2,1)S(1)}, bf16[96,640]{1,0:T(8,128)(2,1)S(1)}, u32[]{:S(2)}, u32[]{:S(2)}) collective-permute-start(bf16[96,640]{1,0:T(8,128)(2,1)S(1)} %get-tuple-element.198), channel_id=1, source_target_pairs={{0,8},{8,0},{16,24},{24,16},{1,9},{9,1},{17,25},{25,17},{2,10},{10... | collective-permute-start | bytes 368648 | tf_op jit(solution)/shard_map/ppermute | solution.py:1181
  381.5 2.3 collective-permute-start.19
  383.9 0.7 slice_dynamic-update-slice_fusion.9
  384.6 0.7 slice_dynamic-update-slice_fusion.8
  385.9 0.7 slice_dynamic-update-slice_fusion.6
  387.3 0.7 slice_dynamic-update-slice_fusion.4
  389.3 0.7 slice_dynamic-update-slice_fusion.1
  390.0 2.6 collective-permute-done.18
  392.6 1.3 multiply_reduce_fusion.1
  395.3 0.7 fusion.36
  396.6 3.6 all-to-all-start
  400.2 0.7 slice_dynamic-update-slice_fusion
  400.8 3.6 collective-permute-start.22
  404.5 0.8 collective-permute-start.20
  405.2 2.1 all-to-all-done
  408.7 4.8 %multiply_subtract_fusion = (f32[64,5096]{1,0:T(8,128)}, f32[64,5096]{1,0:T(8,128)}, f32[64,5096]{1,0:T(8,128)}) fusion(f32[64,5096]{1,0:T(8,128)S(1)} %copy-done.1, f32[64,5120]{1,0:T(8,128)} %slice_dynamic-update-slice_fusion, f32[]{:T(128)S(6)} %min.3, f32[64,5096]{1,0:T(8,128)} %param.36, f32[64,5096]{1,0:T(8,128)} %param.43), kind=kLoop, calls=%fused_computation.9 | loop fusion | flops 5218304 | bytes 9132036 | tf_op jit(solution)/shard_map/sub | solution.py:1237
  413.6 1.9 multiply_subtract_fusion.1
  415.7 1.1 select_select_fusion.7
  418.1 0.7 maximum_convert_fusion.5
  419.0 0.9 reshape.182
  419.9 0.8 mul.492
  423.0 1.6 multiply_subtract_fusion.2
  424.6 1.2 multiply_subtract_fusion.3
  (159 shorter events, 16.7 us)
Async XLA Ops:
  7.2 47.1 %all-gather.11.cloned.1.call-start = ((), (), s32[]{:S(2)}) async-start(), calls=%async_computation.3 | async-start | bytes 4239360 | tf_op jit(solution)/shard_map/all_gather | solution.py:1248
  8.3 2.3 copy-start.2
  9.6 1.9 copy-start
  9.7 0.8 copy-start.7
  10.5 121.7 %all-gather.9.cloned.1.call-start = ((), (), s32[]{:S(2)}) async-start(), calls=%async_computation.2 | async-start | bytes 3833856 | tf_op jit(solution)/shard_map/all_gather | solution.py:1267
  11.4 1.0 copy-start.30
  11.4 2.3 copy-start.24
  11.4 2.3 copy-start.22
  11.5 2.3 copy-start.18
  11.5 120.8 %all-gather.7.cloned.1.call-start = ((), (), s32[]{:S(2)}) async-start(), calls=%async_computation.1 | async-start | bytes 5898240 | tf_op jit(solution)/shard_map/all_gather | solution.py:1268
  26.4 103.9 %collective-permute-start.2 = (f32[8,128]{1,0:T(8,128)S(1)}, f32[8,128]{1,0:T(8,128)S(1)}, u32[]{:S(2)}, u32[]{:S(2)}) collective-permute-start(f32[8,128]{1,0:T(8,128)S(1)} %broadcast_in_dim.19), channel_id=1, source_target_pairs={{0,24},{8,16},{16,8},{24,0},{1,25},{9,17},{17,9},{25,1},{2,26},{10... | collective-permute-start | bytes 12296 | tf_op jit(solution)/shard_map/ppermute | solution.py:1181
  29.8 100.5 %collective-permute-start.1 = (f32[8,128]{1,0:T(8,128)S(1)}, f32[8,128]{1,0:T(8,128)S(1)}, u32[]{:S(2)}, u32[]{:S(2)}) collective-permute-start(f32[8,128]{1,0:T(8,128)S(1)} %broadcast_in_dim.19), channel_id=1, source_target_pairs={{0,16},{8,24},{16,0},{24,8},{1,17},{9,25},{17,1},{25,9},{2,18},{10... | collective-permute-start | bytes 12296 | tf_op jit(solution)/shard_map/ppermute | solution.py:1181
  29.8 100.5 %collective-permute-start = (f32[8,128]{1,0:T(8,128)S(1)}, f32[8,128]{1,0:T(8,128)S(1)}, u32[]{:S(2)}, u32[]{:S(2)}) collective-permute-start(f32[8,128]{1,0:T(8,128)S(1)} %broadcast_in_dim.19), channel_id=1, source_target_pairs={{0,8},{8,0},{16,24},{24,16},{1,9},{9,1},{17,25},{25,17},{2,10},{10... | collective-permute-start | bytes 12296 | tf_op jit(solution)/shard_map/ppermute | solution.py:1181
  201.5 7.8 %collective-permute-start.3 = (bf16[4,1056,512]{2,1,0:T(8,128)(2,1)}, bf16[4,1056,512]{2,1,0:T(8,128)(2,1)}, u32[]{:S(2)}, u32[]{:S(2)}) collective-permute-start(bf16[4,1056,512]{2,1,0:T(8,128)(2,1)} %get-tuple-element.99), channel_id=1, source_target_pairs={{0,1},{1,0},{2,3},{3,2},{4,5},{5,4},{6,7},{7,6},{8,9},{9,8},{10,11... | collective-permute-start | bytes 12976136 | tf_op jit(solution)/shard_map/ppermute | solution.py:1181
  214.4 70.4 %collective-permute-start.4 = (bf16[1056,512]{1,0:T(8,128)(2,1)}, bf16[1056,512]{1,0:T(8,128)(2,1)}, u32[]{:S(2)}, u32[]{:S(2)}) collective-permute-start(bf16[1056,512]{1,0:T(8,128)(2,1)} %get-tuple-element.111), channel_id=1, source_target_pairs={{0,2},{1,3},{2,0},{3,1},{4,6},{5,7},{6,4},{7,5},{8,10},{9,11},{10,... | collective-permute-start | bytes 3244040 | tf_op jit(solution)/shard_map/ppermute | solution.py:1181
  215.5 69.3 %collective-permute-start.5 = (bf16[1056,512]{1,0:T(8,128)(2,1)}, bf16[1056,512]{1,0:T(8,128)(2,1)}, u32[]{:S(2)}, u32[]{:S(2)}) collective-permute-start(bf16[1056,512]{1,0:T(8,128)(2,1)} %get-tuple-element.112), channel_id=1, source_target_pairs={{0,4},{1,5},{2,6},{3,7},{4,0},{5,1},{6,2},{7,3},{8,12},{9,13},{10,... | collective-permute-start | bytes 3244040 | tf_op jit(solution)/shard_map/ppermute | solution.py:1181
  216.4 68.4 %collective-permute-start.6 = (bf16[1056,512]{1,0:T(8,128)(2,1)}, bf16[1056,512]{1,0:T(8,128)(2,1)}, u32[]{:S(2)}, u32[]{:S(2)}) collective-permute-start(bf16[1056,512]{1,0:T(8,128)(2,1)} %get-tuple-element.113), channel_id=1, source_target_pairs={{0,6},{1,7},{2,4},{3,5},{4,2},{5,3},{6,0},{7,1},{8,14},{9,15},{10,... | collective-permute-start | bytes 3244040 | tf_op jit(solution)/shard_map/ppermute | solution.py:1181
  289.7 48.5 %collective-permute-start.7 = (bf16[264,512]{1,0:T(8,128)(2,1)}, bf16[264,512]{1,0:T(8,128)(2,1)}, u32[]{:S(2)}, u32[]{:S(2)}) collective-permute-start(bf16[264,512]{1,0:T(8,128)(2,1)} %get-tuple-element.138), channel_id=1, source_target_pairs={{0,8},{8,0},{16,24},{24,16},{1,9},{9,1},{17,25},{25,17},{2,10},{10... | collective-permute-start | bytes 811016 | tf_op jit(solution)/shard_map/ppermute | solution.py:1181
  290.7 47.5 %collective-permute-start.8 = (bf16[264,512]{1,0:T(8,128)(2,1)}, bf16[264,512]{1,0:T(8,128)(2,1)}, u32[]{:S(2)}, u32[]{:S(2)}) collective-permute-start(bf16[264,512]{1,0:T(8,128)(2,1)} %get-tuple-element.139), channel_id=1, source_target_pairs={{0,16},{8,24},{16,0},{24,8},{1,17},{9,25},{17,1},{25,9},{2,18},{10... | collective-permute-start | bytes 811016 | tf_op jit(solution)/shard_map/ppermute | solution.py:1181
  293.5 44.6 %collective-permute-start.9 = (bf16[264,512]{1,0:T(8,128)(2,1)S(1)}, bf16[264,512]{1,0:T(8,128)(2,1)}, u32[]{:S(2)}, u32[]{:S(2)}) collective-permute-start(bf16[264,512]{1,0:T(8,128)(2,1)S(1)} %get-tuple-element.140), channel_id=1, source_target_pairs={{0,24},{8,16},{16,8},{24,0},{1,25},{9,17},{17,9},{25,1},{2,26},{10... | collective-permute-start | bytes 811016 | tf_op jit(solution)/shard_map/ppermute | solution.py:1181
  338.2 4.2 collective-permute-start.10
  342.5 3.2 copy-start.5
  346.4 11.3 %collective-permute-start.16 = (bf16[264,512]{1,0:T(8,128)(2,1)S(1)}, bf16[264,512]{1,0:T(8,128)(2,1)S(1)}, u32[]{:S(2)}, u32[]{:S(2)}) collective-permute-start(bf16[264,512]{1,0:T(8,128)(2,1)S(1)} %get-tuple-element.202), channel_id=1, source_target_pairs={{0,24},{8,16},{16,8},{24,0},{1,25},{9,17},{17,9},{25,1},{2,26},{10... | collective-permute-start | bytes 811016 | tf_op jit(solution)/shard_map/ppermute | solution.py:1181
  349.7 22.2 %collective-permute-start.15 = (bf16[264,512]{1,0:T(8,128)(2,1)S(1)}, bf16[264,512]{1,0:T(8,128)(2,1)S(1)}, u32[]{:S(2)}, u32[]{:S(2)}) collective-permute-start(bf16[264,512]{1,0:T(8,128)(2,1)S(1)} %get-tuple-element.202), channel_id=1, source_target_pairs={{0,16},{8,24},{16,0},{24,8},{1,17},{9,25},{17,1},{25,9},{2,18},{10... | collective-permute-start | bytes 811016 | tf_op jit(solution)/shard_map/ppermute | solution.py:1181
  349.7 22.2 %collective-permute-start.14 = (bf16[264,512]{1,0:T(8,128)(2,1)S(1)}, bf16[264,512]{1,0:T(8,128)(2,1)S(1)}, u32[]{:S(2)}, u32[]{:S(2)}) collective-permute-start(bf16[264,512]{1,0:T(8,128)(2,1)S(1)} %get-tuple-element.202), channel_id=1, source_target_pairs={{0,8},{8,0},{16,24},{24,16},{1,9},{9,1},{17,25},{25,17},{2,10},{10... | collective-permute-start | bytes 811016 | tf_op jit(solution)/shard_map/ppermute | solution.py:1181
  350.8 21.5 %collective-permute-start.11 = (bf16[384,640]{1,0:T(8,128)(2,1)}, bf16[384,640]{1,0:T(8,128)(2,1)S(1)}, u32[]{:S(2)}, u32[]{:S(2)}) collective-permute-start(bf16[384,640]{1,0:T(8,128)(2,1)} %get-tuple-element.150), channel_id=1, source_target_pairs={{0,2},{1,3},{2,0},{3,1},{4,6},{5,7},{6,4},{7,5},{8,10},{9,11},{10,... | collective-permute-start | bytes 1474568 | tf_op jit(solution)/shard_map/ppermute | solution.py:1181
  351.9 20.4 %collective-permute-start.12 = (bf16[384,640]{1,0:T(8,128)(2,1)S(1)}, bf16[384,640]{1,0:T(8,128)(2,1)S(1)}, u32[]{:S(2)}, u32[]{:S(2)}) collective-permute-start(bf16[384,640]{1,0:T(8,128)(2,1)S(1)} %get-tuple-element.151), channel_id=1, source_target_pairs={{0,4},{1,5},{2,6},{3,7},{4,0},{5,1},{6,2},{7,3},{8,12},{9,13},{10,... | collective-permute-start | bytes 1474568 | tf_op jit(solution)/shard_map/ppermute | solution.py:1181
  357.6 17.2 %collective-permute-start.13 = (bf16[384,640]{1,0:T(8,128)(2,1)S(1)}, bf16[384,640]{1,0:T(8,128)(2,1)S(1)}, u32[]{:S(2)}, u32[]{:S(2)}) collective-permute-start(bf16[384,640]{1,0:T(8,128)(2,1)S(1)} %get-tuple-element.152), channel_id=1, source_target_pairs={{0,6},{1,7},{2,4},{3,5},{4,2},{5,3},{6,0},{7,1},{8,14},{9,15},{10,... | collective-permute-start | bytes 1474568 | tf_op jit(solution)/shard_map/ppermute | solution.py:1181
  376.4 13.6 %collective-permute-start.17 = (bf16[96,640]{1,0:T(8,128)(2,1)S(1)}, bf16[96,640]{1,0:T(8,128)(2,1)S(1)}, u32[]{:S(2)}, u32[]{:S(2)}) collective-permute-start(bf16[96,640]{1,0:T(8,128)(2,1)S(1)} %get-tuple-element.198), channel_id=1, source_target_pairs={{0,8},{8,0},{16,24},{24,16},{1,9},{9,1},{17,25},{25,17},{2,10},{10... | collective-permute-start | bytes 368648 | tf_op jit(solution)/shard_map/ppermute | solution.py:1181
  381.5 8.4 %collective-permute-start.19 = (bf16[96,640]{1,0:T(8,128)(2,1)S(1)}, bf16[96,640]{1,0:T(8,128)(2,1)S(1)}, u32[]{:S(2)}, u32[]{:S(2)}) collective-permute-start(bf16[96,640]{1,0:T(8,128)(2,1)S(1)} %get-tuple-element.199), channel_id=1, source_target_pairs={{0,24},{8,16},{16,8},{24,0},{1,25},{9,17},{17,9},{25,1},{2,26},{10... | collective-permute-start | bytes 368648 | tf_op jit(solution)/shard_map/ppermute | solution.py:1181
  383.9 8.7 %collective-permute-start.18 = (bf16[96,640]{1,0:T(8,128)(2,1)S(1)}, bf16[96,640]{1,0:T(8,128)(2,1)S(1)}, u32[]{:S(2)}, u32[]{:S(2)}) collective-permute-start(bf16[96,640]{1,0:T(8,128)(2,1)S(1)} %get-tuple-element.200), channel_id=1, source_target_pairs={{0,16},{8,24},{16,0},{24,8},{1,17},{9,25},{17,1},{25,9},{2,18},{10... | collective-permute-start | bytes 368648 | tf_op jit(solution)/shard_map/ppermute | solution.py:1181
  385.9 22.7 %copy-start.1 = (f32[64,5096]{1,0:T(8,128)S(1)}, f32[64,5096]{1,0:T(8,128)}, u32[]{:S(2)}) copy-start(f32[64,5096]{1,0:T(8,128)} %param.29) | copy-start | bytes 3913732
  396.6 10.8 %all-to-all-start = ((f32[32,1,128]{2,1,0:T(1,128)}), f32[32,1,128]{2,1,0:T(1,128)S(1)}, u32[]{:S(2)}, u32[]{:S(2)}) async-start(f32[32,1,128]{2,1,0:T(1,128)} %broadcast_in_dim.21), calls=%async_computation | async-start | bytes 32768 | tf_op jit(solution)/shard_map/all_to_all | solution.py:1227
  400.8 14.7 %collective-permute-start.22 = (bf16[96,640]{1,0:T(8,128)(2,1)}, bf16[96,640]{1,0:T(8,128)(2,1)}, u32[]{:S(2)}, u32[]{:S(2)}) collective-permute-start(bf16[96,640]{1,0:T(8,128)(2,1)} %get-tuple-element.191), channel_id=1, source_target_pairs={{0,24},{8,16},{16,8},{24,0},{1,25},{9,17},{17,9},{25,1},{2,26},{10... | collective-permute-start | bytes 368648 | tf_op jit(solution)/shard_map/ppermute | solution.py:1181
  404.5 11.3 %collective-permute-start.21 = (bf16[96,640]{1,0:T(8,128)(2,1)}, bf16[96,640]{1,0:T(8,128)(2,1)}, u32[]{:S(2)}, u32[]{:S(2)}) collective-permute-start(bf16[96,640]{1,0:T(8,128)(2,1)} %get-tuple-element.191), channel_id=1, source_target_pairs={{0,16},{8,24},{16,0},{24,8},{1,17},{9,25},{17,1},{25,9},{2,18},{10... | collective-permute-start | bytes 368648 | tf_op jit(solution)/shard_map/ppermute | solution.py:1181
  404.5 11.3 %collective-permute-start.20 = (bf16[96,640]{1,0:T(8,128)(2,1)}, bf16[96,640]{1,0:T(8,128)(2,1)}, u32[]{:S(2)}, u32[]{:S(2)}) collective-permute-start(bf16[96,640]{1,0:T(8,128)(2,1)} %get-tuple-element.191), channel_id=1, source_target_pairs={{0,8},{8,0},{16,24},{24,16},{1,9},{9,1},{17,25},{25,17},{2,10},{10... | collective-permute-start | bytes 368648 | tf_op jit(solution)/shard_map/ppermute | solution.py:1181
  408.7 4.9 %copy-start.3 = (f32[416,512]{1,0:T(8,128)S(1)}, f32[416,512]{1,0:T(8,128)}, u32[]{:S(2)}) copy-start(f32[416,512]{1,0:T(8,128)} %param.30) | copy-start | bytes 2555908
  408.7 4.9 %copy-start.8 = (f32[416,512]{1,0:T(8,128)S(1)}, f32[416,512]{1,0:T(8,128)}, u32[]{:S(2)}) copy-start(f32[416,512]{1,0:T(8,128)} %param.37) | copy-start | bytes 2555908
  408.7 4.9 %copy-start.9 = (f32[416,512]{1,0:T(8,128)S(1)}, f32[416,512]{1,0:T(8,128)}, u32[]{:S(2)}) copy-start(f32[416,512]{1,0:T(8,128)} %param.44) | copy-start | bytes 2555908
  413.6 2.2 copy-start.12
  418.8 2.1 copy-start.23
  418.8 2.7 copy-start.19
  418.8 3.4 copy-start.25
  418.8 4.0 copy-start.4
  418.8 4.0 copy-start.10
  418.9 4.0 copy-start.11
  418.9 2.0 copy-start.26
  419.0 2.0 copy-start.27
  419.0 2.6 copy-start.20
  419.0 2.6 copy-start.21
  419.0 3.2 copy-start.28
  419.0 3.2 copy-start.29
  422.9 1.6 copy-start.6
  422.9 1.6 copy-start.13
  422.9 1.6 copy-start.14
  422.9 1.6 copy-start.15
  422.9 1.6 copy-start.16
  422.9 1.7 copy-start.17
Sparse Core Ops, SparseCore 0:
  10.6 37.7 all-gather.10
  50.9 33.4 all-gather.8
  86.8 41.1 all-gather.6
